TPU v7x, 512 devices: a whole 4x4x16 slice. The times are simulated.
512 devices in a mesh: cube: 32 (over x, z_lo, core), wide: 16 (over z_hi, y).
Axes of the slice: x: 4, y: 4, z: 16 (z_hi: 4, z_lo: 4; z = z_hi * 4 + z_lo), core: 2. Of those that a mesh axis runs over, the one named last changes fastest.
Arguments:
- leaf_updates: float32 [32, 2048, 2048], P('cube', 'wide'), may hold values from -1 to 1, as said below
- level1_entries: float32 [2048, 32, 2, 512], P('wide', 'cube'), may hold values from -1 to 1, as said below
- level2_entries: float32 [2048, 32, 512], P('wide', 'cube'), may hold values from -1 to 97, as said below
- leaf_maps: int32 [32, 2048], replicated, may hold values from 0 to 2047, as said below
- leaf_live: int32 [32, 16], replicated, may hold values from 32 to 128
- parent_maps: int32 [16, 2048], replicated, may hold values from 0 to 2047, as said below
- parent_live: int32 [16, 16], replicated, may hold values from 32 to 128
Outputs:
- panel_factor: float32 [32, 512, 128], P('cube', 'wide')
- schur_rows: float32 [2048, 32, 512], P('wide', 'cube')
Inputs may be any that keep to these rules, and one draw needn't show every extreme that they name: Within each index block, leaf_maps[c, b * 128 to (b + 1) * 128 - 1] is a permutation of the same range of indices. Within each index block, parent_maps[p, b * 128 to (b + 1) * 128 - 1] is a permutation of the same range of indices. `leaf_updates`: each leaf update matrix is symmetric. `level1_entries`: each level-1 front's initial entries form a symmetric matrix. `level2_entries`: each level-2 front's initial entries form a symmetric matrix; its diagonal entries at the indices of P are at least 47.
All inputs are finite; a program needn't handle non-finite values.
Results may differ from a plain program's by a relative error of at most 0.0003.
Values sent between devices are 32-bit elements; how exact they have to be, the bound alone decides.
A program may use at most 64 MiB of HBM per device.

v0:
```python
import jax
import jax.numpy as jnp
from jax import lax
from jax.sharding import PartitionSpec as P

CYCLIC = 8
PANEL = 128


HIGHEST = lax.Precision.HIGHEST


def from_partner(array, axis, stride):
    return lax.ppermute(array, axis, [(i, i ^ 1 << stride) for i in range(lax.axis_size(axis))])


def block_onehot(offsets_map, live_amounts, block_rows):
    block_count = offsets_map.shape[0] // block_rows
    offsets = (
        offsets_map.reshape(block_count, block_rows)
        - (jnp.arange(block_count, dtype=jnp.int32) * block_rows)[:, None]
    )
    living = jnp.arange(block_rows, dtype=jnp.int32)[None, :] < live_amounts[:, None]
    matched = (
        offsets[:, :, None] == jnp.arange(block_rows, dtype=jnp.int32)[None, None, :]
    ) & living[:, :, None]
    return matched.astype(jnp.float32)


def select_row(lookup, position):
    return lax.dynamic_index_in_dim(lookup, position, 0, keepdims=False)


def map_columns(mapped_rows, onehot_sel):
    return jnp.einsum("rhnj,hnjk->rhnk", mapped_rows, onehot_sel, precision=HIGHEST)


def join_halves(mine, received, upper):
    lower_first = jnp.concatenate((mine, received), axis=1)
    upper_first = jnp.concatenate((received, mine), axis=1)
    return jnp.where(upper == 1, upper_first, lower_first)


def on_device(
    leaf_updates, level1_entries, level2_entries, leaf_maps, leaf_live, parent_maps, parent_live
):
    wide_count = lax.axis_size("wide")
    cube_index = lax.axis_index("cube")
    wide_index = lax.axis_index("wide")
    block_rows = leaf_updates.shape[1]
    front_order = leaf_updates.shape[2]
    quarter_cols = front_order // 4
    quarter_blocks = quarter_cols // block_rows
    pivot_share = PANEL // 4
    low_bit = cube_index % 2
    high_bit = cube_index // 2 % 2
    quarter = cube_index % 4
    own_update = leaf_updates[0]

    def leaf_columns(onehot, mapped_rows, column_half):
        chosen_rows = lax.dynamic_index_in_dim(mapped_rows, column_half, 2, keepdims=False)
        chosen_hot = lax.dynamic_index_in_dim(
            onehot.reshape(2, 2, quarter_blocks, block_rows, block_rows),
            column_half,
            1,
            keepdims=False,
        )
        return map_columns(chosen_rows, chosen_hot).reshape(block_rows, 2, quarter_cols)

    own_hot = block_onehot(
        select_row(leaf_maps, cube_index), select_row(leaf_live, cube_index), block_rows
    )
    mapped = jnp.dot(select_row(own_hot, wide_index).T, own_update, precision=HIGHEST)
    own_rows = mapped.reshape(block_rows, 2, 2, quarter_blocks, block_rows)
    first_front = level1_entries[:, 0] + leaf_columns(own_hot, own_rows, low_bit)
    outgoing = leaf_columns(own_hot, own_rows, 1 - low_bit)
    first_front = first_front + from_partner(outgoing, "cube", 0)
    parent_index = cube_index // 2
    upper_hot = block_onehot(
        select_row(parent_maps, parent_index), select_row(parent_live, parent_index), block_rows
    )
    upper_rows = jnp.dot(
        select_row(upper_hot, wide_index).T,
        first_front.reshape(block_rows, 2 * quarter_cols),
        precision=HIGHEST,
    )
    upper_rows = upper_rows.reshape(block_rows, 2, quarter_blocks, block_rows)
    upper_sel = lax.dynamic_index_in_dim(
        upper_hot.reshape(2, 2, quarter_blocks, block_rows, block_rows), low_bit, 1, keepdims=False
    )
    upper_mapped = map_columns(upper_rows, upper_sel).reshape(block_rows, 2, quarter_cols)
    kept_quarter = lax.dynamic_index_in_dim(upper_mapped, high_bit, 1, keepdims=False)
    given_quarter = lax.dynamic_index_in_dim(upper_mapped, 1 - high_bit, 1, keepdims=False)
    second_front = level2_entries[:, 0] + kept_quarter + from_partner(given_quarter, "cube", 1)
    span_count = block_rows // (CYCLIC * wide_count)
    local_rows = jnp.arange(block_rows, dtype=jnp.int32)
    second_front = lax.all_to_all(
        jnp.transpose(
            second_front.reshape(span_count, wide_count, CYCLIC, quarter_cols), (1, 0, 2, 3)
        ),
        "wide",
        split_axis=0,
        concat_axis=0,
        tiled=True,
    ).reshape(block_rows, quarter_cols)
    raw_panel = second_front[:, :pivot_share]
    gathered = lax.all_gather(raw_panel, "wide", axis=0, tiled=True)
    for level in range(2):
        received = from_partner(gathered, "cube", level)
        gathered = join_halves(gathered, received, cube_index // 2**level % 2)

    def to_natural(layout_rows):
        shaped = layout_rows.reshape(wide_count, wide_count, span_count, CYCLIC, PANEL)
        return jnp.transpose(shaped, (1, 2, 0, 3, 4)).reshape(front_order, PANEL)

    natural_cols = to_natural(gathered)
    pivot_rows = natural_cols.reshape(4, quarter_cols, PANEL)[:, :pivot_share].reshape(PANEL, PANEL)
    pivot_block = jnp.linalg.cholesky(pivot_rows)
    layout_solved = lax.linalg.triangular_solve(
        pivot_block, gathered, left_side=False, lower=True, transpose_a=True
    )
    natural_solved = to_natural(layout_solved)
    mine_solved = select_row(layout_solved.reshape(wide_count, block_rows, PANEL), wide_index)
    column_solved = lax.dynamic_slice_in_dim(
        natural_solved, quarter * quarter_cols, quarter_cols, 0
    )
    schur_local = second_front - jnp.dot(mine_solved, column_solved.T, precision=HIGHEST)
    source_part = local_rows // (span_count * CYCLIC)
    span_part = local_rows // CYCLIC % span_count
    global_rows = (
        source_part * (block_rows // CYCLIC) + span_part * wide_count + wide_index
    ) * CYCLIC + local_rows % CYCLIC
    row_outside = global_rows % quarter_cols >= pivot_share
    col_outside = jnp.arange(quarter_cols, dtype=jnp.int32) >= pivot_share
    kept_mask = row_outside[:, None] & col_outside[None, :]
    schur_local = jnp.where(kept_mask, schur_local, jnp.zeros_like(schur_local))
    share_rows = quarter_cols // wide_count
    panel_local = lax.dynamic_slice_in_dim(column_solved, wide_index * share_rows, share_rows, 0)
    return (panel_local[None], schur_local[:, None, :])


def solution(mesh):
    placed = (
        P("cube", "wide", None),
        P("wide", "cube", None, None),
        P("wide", "cube", None),
        P(),
        P(),
        P(),
        P(),
    )
    return jax.shard_map(
        on_device,
        mesh=mesh,
        in_specs=placed,
        out_specs=(P("cube", "wide", None), P("wide", "cube", None)),
        check_vma=False,
    )
```

profile of v0, /device:TPU:1, one launch (start us, length us, event | category | flops | bytes accessed | tf_op | source)
XLA Modules:
  0.0 179.6 jit_solution(6087372789219417100)
XLA Ops:
  0.7 0.7 copy-done.6
  1.8 0.9 constant_dynamic-slice_fusion.10
  2.6 0.7 fusion.58
  3.4 1.5 copy.82
  7.0 8.8 %collective-permute-start = (f32[128,2,512]{2,1,0:T(2,128)S(1)}, f32[128,2,512]{2,1,0:T(2,128)}, u32[]{:S(2)}, u32[]{:S(2)}) collective-permute-start(f32[128,2,512]{2,1,0:T(2,128)S(1)} %copy.64), channel_id=1, source_target_pairs={{0,16},{16,0},{32,48},{48,32},{64,80},{80,64},{96,112},{112,96},{1... | collective-permute-start | bytes 1572872 | tf_op jit(solution)/shard_map/ppermute | solution.py:14
  17.5 1.4 fusion.15
  20.5 1.9 %collective-permute-start.1 = (f32[128,512]{1,0:T(8,128)S(1)}, f32[128,512]{1,0:T(8,128)S(1)}, u32[]{:S(2)}, u32[]{:S(2)}) collective-permute-start(f32[128,512]{1,0:T(8,128)S(1)} %bitcast.118), channel_id=1, source_target_pairs={{0,32},{16,48},{32,0},{48,16},{64,96},{80,112},{96,64},{112,80},{1... | collective-permute-start | bytes 786440 | tf_op jit(solution)/shard_map/ppermute | solution.py:14
  22.6 0.8 copy-done.5
  23.7 6.4 %collective-permute-done.1 = f32[128,512]{1,0:T(8,128)S(1)} collective-permute-done((f32[128,512]{1,0:T(8,128)S(1)}, f32[128,512]{1,0:T(8,128)S(1)}, u32[]{:S(2)}, u32[]{:S(2)}) %collective-permute-start.1) | collective-permute-done | bytes 262176 | tf_op jit(solution)/shard_map/ppermute | solution.py:14
  30.1 27.1 %all_to_all.5 = f32[16,1,8,512]{3,2,1,0:T(8,128)S(1)} all-to-all(f32[16,1,8,512]{3,2,1,0:T(8,128)S(1)} %fusion.28), channel_id=1, replica_groups=mesh['cube'=32,'wide'=16] {'wide'}, dimensions={0} | all-to-all | bytes 524288 | tf_op jit(solution)/shard_map/all_to_all | solution.py:97
  57.2 0.7 copy-done.2
  57.9 61.8 %all_gather.3 = f32[2048,32]{1,0:T(8,128)S(1)} all-gather(f32[128,32]{1,0:T(8,128)S(1)} %slice.18), channel_id=1, replica_groups=mesh['cube'=32,'wide'=16] {'wide'}, dimensions={0}, use_global_device_ids=true | all-gather | bytes 278528 | tf_op jit(solution)/shard_map/all_gather | solution.py:107
  120.0 11.7 %collective-permute-start.2 = (f32[2048,32]{0,1:T(8,128)S(1)}, f32[2048,32]{0,1:T(8,128)S(1)}, u32[]{:S(2)}, u32[]{:S(2)}) collective-permute-start(f32[2048,32]{0,1:T(8,128)S(1)} %copy.68), channel_id=1, source_target_pairs={{0,16},{16,0},{32,48},{48,32},{64,80},{80,64},{96,112},{112,96},{1... | collective-permute-start | bytes 786440 | tf_op jit(solution)/shard_map/ppermute | solution.py:14
  131.7 1.1 collective-permute-done.2
  133.8 1.1 copy.71
  135.0 2.5 %collective-permute-start.3 = (f32[2048,64]{0,1:T(8,128)}, f32[2048,64]{0,1:T(8,128)}, u32[]{:S(2)}, u32[]{:S(2)}) collective-permute-start(f32[2048,64]{0,1:T(8,128)} %copy.71), channel_id=1, source_target_pairs={{0,32},{16,48},{32,0},{48,16},{64,96},{80,112},{96,64},{112,80},{1... | collective-permute-start | bytes 1572872 | tf_op jit(solution)/shard_map/ppermute | solution.py:14
  137.5 1.6 fusion.8
  139.1 11.2 %collective-permute-done.3 = f32[2048,64]{0,1:T(8,128)} collective-permute-done((f32[2048,64]{0,1:T(8,128)}, f32[2048,64]{0,1:T(8,128)}, u32[]{:S(2)}, u32[]{:S(2)}) %collective-permute-start.3) | collective-permute-done | bytes 524320 | tf_op jit(solution)/shard_map/ppermute | solution.py:14
  150.3 1.4 copy.72
  152.5 11.7 %cholesky.16 = f32[128,128]{1,0:T(8,128)S(1)} custom-call(f32[128,128]{1,0:T(8,128)S(1)} %fusion.34), custom_call_target="Cholesky" | custom-call | tf_op jit(solution)/shard_map/jit(cholesky)/cholesky | solution.py:118
  165.6 9.8 %custom-call.6 = f32[1,128,128]{1,2,0:T(8,128)S(1)} custom-call(f32[1,128,128]{2,1,0:T(8,128)S(1)} %fusion.31), custom_call_target="InvertDiagBlocksLowerTriangular" | custom-call | tf_op jit(solution)/shard_map/triangular_solve | solution.py:119
  175.4 1.3 fusion.2
  176.8 0.8 copy-done.3
  178.0 1.0 copy.79
  (61 shorter events, 10.6 us)
Async XLA Ops:
  0.6 1.1 copy-start
  0.7 0.7 copy-start.6
  7.0 10.4 %collective-permute-start = (f32[128,2,512]{2,1,0:T(2,128)S(1)}, f32[128,2,512]{2,1,0:T(2,128)}, u32[]{:S(2)}, u32[]{:S(2)}) collective-permute-start(f32[128,2,512]{2,1,0:T(2,128)S(1)} %copy.64), channel_id=1, source_target_pairs={{0,16},{16,0},{32,48},{48,32},{64,80},{80,64},{96,112},{112,96},{1... | collective-permute-start | bytes 1572872 | tf_op jit(solution)/shard_map/ppermute | solution.py:14
  16.5 1.0 copy-start.4
  20.5 9.5 %collective-permute-start.1 = (f32[128,512]{1,0:T(8,128)S(1)}, f32[128,512]{1,0:T(8,128)S(1)}, u32[]{:S(2)}, u32[]{:S(2)}) collective-permute-start(f32[128,512]{1,0:T(8,128)S(1)} %bitcast.118), channel_id=1, source_target_pairs={{0,32},{16,48},{32,0},{48,16},{64,96},{80,112},{96,64},{112,80},{1... | collective-permute-start | bytes 786440 | tf_op jit(solution)/shard_map/ppermute | solution.py:14
  22.4 1.0 copy-start.5
  57.2 0.7 copy-start.2
  120.0 12.8 %collective-permute-start.2 = (f32[2048,32]{0,1:T(8,128)S(1)}, f32[2048,32]{0,1:T(8,128)S(1)}, u32[]{:S(2)}, u32[]{:S(2)}) collective-permute-start(f32[2048,32]{0,1:T(8,128)S(1)} %copy.68), channel_id=1, source_target_pairs={{0,16},{16,0},{32,48},{48,32},{64,80},{80,64},{96,112},{112,96},{1... | collective-permute-start | bytes 786440 | tf_op jit(solution)/shard_map/ppermute | solution.py:14
  135.0 15.3 %collective-permute-start.3 = (f32[2048,64]{0,1:T(8,128)}, f32[2048,64]{0,1:T(8,128)}, u32[]{:S(2)}, u32[]{:S(2)}) collective-permute-start(f32[2048,64]{0,1:T(8,128)} %copy.71), channel_id=1, source_target_pairs={{0,32},{16,48},{32,0},{48,16},{64,96},{80,112},{96,64},{112,80},{1... | collective-permute-start | bytes 1572872 | tf_op jit(solution)/shard_map/ppermute | solution.py:14
  139.1 12.6 %copy-start.1 = (f32[16,16,1,8,64]{4,3,1,0,2:T(8,128)S(1)}, f32[16,16,1,8,64]{4,3,1,0,2:T(8,128)}, u32[]{:S(2)}) copy-start(f32[16,16,1,8,64]{4,3,1,0,2:T(8,128)} %fusion.8) | copy-start | bytes 1572868
  176.7 1.0 copy-start.3
where the time goes:
time: 183 us; the launch traced here: 180 us
  blocking collectives  89 us (49%)
  other arithmetic  28 us (15%)
  starting transfers between devices  24.9 us (14%)
  waiting for transfers between devices  19.2 us (10%)
  local copies, waits for them, and re-layouts  12.7 us (7%)
  matrix products  4.72 us (3%)
    all_gather x1, blocking collectives, on_device(): gathered = lax.all_gather(raw_panel, 'wide', axis=0, tiled=True)  61.8 us
    all_to_all x1, blocking collectives, on_device(): lax.all_to_all(jnp.transpose(second_front.reshape(span_count, wide_count,...  27.1 us
    ppermute x4, starting transfers between devices, from_partner(): lax.ppermute(array, axis, [(i, i ^ 1 << stride) for i in range(lax.axis_s...  24.9 us
    ppermute x4, waiting for transfers between devices, from_partner(): lax.ppermute(array, axis, [(i, i ^ 1 << stride) for i in range(lax.axis_s...  19.2 us
    another operation x3, other arithmetic, on_device(): pivot_block = jnp.linalg.cholesky(pivot_rows)  12.4 us
    another operation x2, other arithmetic, on_device(): lax.linalg.triangular_solve(pivot_block, gathered, left_side=False, lower...  10.5 us
    unnamed x17, local copies, waits for them, and re-layouts  4.36 us
  transfers between devices with their start and end apart: 4, of which 4 were waited for; matrix products, arithmetic and copies ran while one was open for 2% of the time, Pallas kernels for 0%

commit v1 on v0

v1 whole, which is shorter than its diff:
```python
import jax
import jax.numpy as jnp
from jax import lax
from jax.experimental import pallas as pl
from jax.experimental.pallas import tpu as pltpu
from jax.sharding import PartitionSpec as P

F32 = jnp.float32
BF16 = jnp.bfloat16
MESH = pl.DeviceIdType.MESH
HIGHEST = lax.Precision.HIGHEST
B = 128
Q = 512
PIV = 32
CYC = 8


def iota(shape, dim):
    return lax.broadcasted_iota(jnp.int32, shape, dim)


def kernel(
    x_hbm, l1_hbm, l2_hbm, lm_hbm, ll_hbm, pm_hbm, pv_hbm,
    panel_hbm, schur_hbm,
    x_v, l1_v, l2_v, lm_v, pm_v, ll_s, pv_s,
    zs, zo, zr, us, uk, ur, f2, f2r, at, lt, msg, msgs, mat, linv, tr_v, out_v, panel_v,
    in_sem, e1_send, e1_recv, e2_send, e2_recv, aa_send, aa_recv,
    sc_send, sc_recv, zg_send, yg_send, pg_recv, cb_send, cb_recv, out_sem,
):
    cube = lax.axis_index("cube")
    wide = lax.axis_index("wide")
    low = cube % 2
    high = cube // 2 % 2
    quarter = cube % 4
    group = cube - quarter
    z_hi = wide // 4
    y = wide % 4
    parent = cube // 2

    lm_base = pl.multiple_of(cube // 8 * 8, 8)
    pm_base = pl.multiple_of(parent // 8 * 8, 8)
    loads = [
        pltpu.make_async_copy(lm_hbm.at[pl.ds(lm_base, 8)], lm_v, in_sem.at[0]),
        pltpu.make_async_copy(ll_hbm, ll_s, in_sem.at[1]),
        pltpu.make_async_copy(x_hbm.at[0], x_v, in_sem.at[2]),
        pltpu.make_async_copy(l1_hbm, l1_v, in_sem.at[3]),
        pltpu.make_async_copy(pm_hbm.at[pl.ds(pm_base, 8)], pm_v, in_sem.at[4]),
        pltpu.make_async_copy(pv_hbm, pv_s, in_sem.at[5]),
        pltpu.make_async_copy(l2_hbm, l2_v, in_sem.at[6]),
    ]
    for load in loads:
        load.start()

    barrier = pltpu.get_barrier_semaphore()
    for d in range(1, 4):
        pl.semaphore_signal(barrier, inc=1, device_id=(cube ^ d, wide), device_id_type=MESH)

    @pl.loop(1, 16)
    def _(d):
        pl.semaphore_signal(barrier, inc=1, device_id=(cube, (wide + d) % 16), device_id_type=MESH)

    def one_hot(map_ref, live_ref, live_row, block):
        lanes = pl.multiple_of(block * B, B)
        entry = map_ref[:1, pl.ds(lanes, B)] - lanes
        live = live_ref[block, live_row] if live_ref is ll_s else live_ref[live_row, block]
        hit = (entry == iota((B, B), 0)) & (iota((B, B), 1) < live)
        return jnp.where(hit, 1.0, 0.0).astype(BF16)

    def map_quarter(values, row_hot, hots):
        top = values.astype(BF16)
        rest = (values - top.astype(F32)).astype(BF16)
        top = jnp.dot(row_hot, top, preferred_element_type=F32).astype(BF16)
        rest = jnp.dot(row_hot, rest, preferred_element_type=F32).astype(BF16)
        parts = []
        for i in range(4):
            both = jnp.concatenate((top[:, i * B : (i + 1) * B], rest[:, i * B : (i + 1) * B]), axis=0)
            got = lax.dot_general(both, hots[i], (((1,), (1,)), ((), ())), preferred_element_type=F32)
            parts.append(got[:B] + got[B:])
        return jnp.concatenate(parts, axis=1)

    loads[0].wait()
    loads[1].wait()
    lm_v[:1, :] = lm_v[pl.ds(cube - lm_base, 1), :]
    row_hot = one_hot(lm_v, ll_s, cube, wide)
    loads[2].wait()

    def leaf_quarter(at_quarter):
        hots = [one_hot(lm_v, ll_s, cube, at_quarter * 4 + i) for i in range(4)]
        values = x_v[:, pl.ds(pl.multiple_of(at_quarter * Q, Q), Q)]
        return map_quarter(values, row_hot, hots)

    def exchange1(n):
        return pltpu.make_async_remote_copy(
            src_ref=zs.at[n], dst_ref=zr.at[n], send_sem=e1_send.at[n], recv_sem=e1_recv.at[n],
            device_id=(cube ^ 1, wide), device_id_type=MESH,
        )

    for n in range(2):
        half = 1 - high if n == 0 else high
        zs[n] = leaf_quarter(2 * half + 1 - low)
        if n == 0:
            pl.semaphore_wait(barrier, 18)
        exchange1(n).start()
    for n in range(2):
        half = 1 - high if n == 0 else high
        zo[n] = leaf_quarter(2 * half + low)

    for n in range(3, 7):
        loads[n].wait()
    pm_v[:1, :] = pm_v[pl.ds(parent - pm_base, 1), :]
    up_row_hot = one_hot(pm_v, pv_s, parent, wide)

    def upper_quarter(n):
        half = 1 - high if n == 0 else high
        first = jnp.where(half == 0, l1_v[:, 0, 0, :], l1_v[:, 0, 1, :])
        values = first + zo[n] + zr[n]
        hots = [one_hot(pm_v, pv_s, parent, (2 * half + low) * 4 + i) for i in range(4)]
        return map_quarter(values, up_row_hot, hots)

    def exchange2(i):
        rows = pl.ds(pl.multiple_of(i * 32, 32), 32)
        return pltpu.make_async_remote_copy(
            src_ref=us.at[rows], dst_ref=ur.at[rows], send_sem=e2_send.at[i], recv_sem=e2_recv.at[i],
            device_id=(cube ^ 2, wide), device_id_type=MESH,
        )

    exchange1(0).wait_recv()
    us[...] = upper_quarter(0)
    exchange2(0).start()
    order = (2, 1, 3, 0)
    for o in order:
        chunk = (z_hi + o) % 4

        @pl.when(chunk != 0)
        def _():
            exchange2(chunk).start()

    exchange1(1).wait_recv()
    uk[...] = upper_quarter(1) + l2_v[:, 0, :]

    def finish_chunk(i):
        exchange2(i).wait_recv()
        rows = pl.ds(pl.multiple_of(i * 32, 32), 32)
        f2[rows, :] = uk[rows, :] + ur[rows, :]

    def rows_of(w):
        return pl.ds(pl.multiple_of(w * CYC, CYC), CYC)

    def spread(w):
        return pltpu.make_async_remote_copy(
            src_ref=f2.at[rows_of(w)], dst_ref=f2r.at[rows_of(wide)],
            send_sem=aa_send.at[w], recv_sem=aa_recv.at[wide],
            device_id=(cube, w), device_id_type=MESH,
        )

    def spread_from(w):
        return pltpu.make_async_remote_copy(
            src_ref=f2.at[rows_of(w)], dst_ref=f2r.at[rows_of(w)],
            send_sem=aa_send.at[w], recv_sem=aa_recv.at[w],
            device_id=(cube, w), device_id_type=MESH,
        )

    finish_chunk(0)

    def scatter(j):
        return pltpu.make_async_remote_copy(
            src_ref=f2.at[pl.ds(j * CYC, CYC)], dst_ref=at.at[rows_of(4 * z_hi + j)],
            send_sem=sc_send.at[j], recv_sem=sc_recv.at[0],
            device_id=(cube, 4 * z_hi + j), device_id_type=MESH,
        )

    def along_z(d):
        return pltpu.make_async_remote_copy(
            src_ref=at.at[rows_of(wide)], dst_ref=at.at[rows_of(wide)],
            send_sem=zg_send.at[d], recv_sem=pg_recv.at[wide],
            device_id=(cube, (wide + 4 * d) % 16), device_id_type=MESH,
        )

    def along_y(piece_z, d):
        piece = 4 * piece_z + y
        return pltpu.make_async_remote_copy(
            src_ref=at.at[rows_of(piece)], dst_ref=at.at[rows_of(piece)],
            send_sem=yg_send.at[piece_z, d], recv_sem=pg_recv.at[piece],
            device_id=(cube, 4 * z_hi + (y + d) % 4), device_id_type=MESH,
        )

    def piece_from(piece):
        return pltpu.make_async_remote_copy(
            src_ref=at.at[rows_of(piece)], dst_ref=at.at[rows_of(piece)],
            send_sem=zg_send.at[0], recv_sem=pg_recv.at[piece],
            device_id=(cube, piece), device_id_type=MESH,
        )

    @pl.when(y == 0)
    def _():
        for j in range(1, 4):
            scatter(j).start()
        at[rows_of(wide), :] = f2[:CYC, :]

    @pl.when(y != 0)
    def _():
        pltpu.make_async_remote_copy(
            src_ref=f2.at[pl.ds(0, CYC)], dst_ref=at.at[rows_of(wide)],
            send_sem=sc_send.at[0], recv_sem=sc_recv.at[0],
            device_id=(cube, 4 * z_hi), device_id_type=MESH,
        ).wait_recv()

    for d in (2, 1, 3):
        along_z(d).start()
    for d in (2, 1, 3):
        along_y(z_hi, d).start()

    for o in order:
        chunk = (z_hi + o) % 4

        @pl.when(chunk != 0)
        def _():
            finish_chunk(chunk)

        for k in range(4):
            w = 4 * chunk + k

            @pl.when(w != wide)
            def _():
                spread(w).start()

    f2r[rows_of(wide), :] = f2[rows_of(wide), :]

    for o in (1, 3, 2):
        piece_z = (z_hi + o) % 4
        piece_from(4 * piece_z + y).wait_recv()
        for d in (2, 1, 3):
            along_y(piece_z, d).start()

    @pl.loop(0, 16)
    def _(piece):
        @pl.when(piece % 4 != y)
        def _():
            piece_from(piece).wait_recv()

    lane = iota((B, B), 1)
    packed = at[:, :B]
    for i in range(4):
        shift = (PIV + CYC * i - CYC * wide + B) % B
        moved = pltpu.roll(at[:, i * B : (i + 1) * B], shift, 1)
        packed = jnp.where((lane >= PIV + CYC * i) & (lane < PIV + CYC * (i + 1)), moved, packed)
    msg[...] = jnp.where(lane[:64] < 64, packed[:64], pltpu.roll(packed[64:], 64, 1))

    def share(d):
        return pltpu.make_async_remote_copy(
            src_ref=msg, dst_ref=msgs.at[quarter], send_sem=cb_send.at[d], recv_sem=cb_recv.at[quarter],
            device_id=(cube ^ d, wide), device_id_type=MESH,
        )

    for d in range(1, 4):
        share(d).start()
    msgs[quarter] = msg[...]

    for d in range(1, 4):
        other = quarter ^ d
        pltpu.make_async_remote_copy(
            src_ref=msg, dst_ref=msgs.at[other], send_sem=cb_send.at[d], recv_sem=cb_recv.at[other],
            device_id=(group + other, wide), device_id_type=MESH,
        ).wait_recv()

    def unpack(first_lane):
        got = jnp.zeros((64, B), F32)
        for i in range(4):
            moved = pltpu.roll(msgs[i], (PIV * i - first_lane) % B, 1)
            got = jnp.where((lane[:64] >= PIV * i) & (lane[:64] < PIV * (i + 1)), moved, got)
        return got

    mat[:64, :B] = unpack(0)
    mat[64:, :B] = unpack(64)
    rows_t = jnp.concatenate((unpack(32), unpack(96)), axis=0)
    mat[:, B:] = jnp.where(iota((B, B), 0) == lane, 1.0, 0.0)

    @pl.loop(0, 4)
    def _(step):
        left = mat[:PIV, :B]
        right = mat[:PIV, B:]
        row_id = iota((PIV, 1), 0)
        diag = jnp.ones((PIV, 1), F32)
        for j in range(PIV):
            pivot = left[j : j + 1, j : j + 1]
            column = left[:, j : j + 1]
            diag = jnp.where(row_id == j, pivot, diag)
            factor = jnp.where(row_id > j, column * (1.0 / pivot), 0.0)
            left = left - factor * left[j : j + 1, :]
            right = right - factor * right[j : j + 1, :]
        scale = lax.rsqrt(diag)
        left = pltpu.roll(left * scale, B - PIV, 1)
        left = jnp.where(lane[:PIV] < B - PIV, left, 0.0)
        right = right * scale
        linv[pl.ds(pl.multiple_of(step * PIV, PIV), PIV), :] = right
        both = jnp.concatenate((left, right), axis=1)
        change = lax.dot_general(
            left, both, (((0,), (0,)), ((), ())), precision=HIGHEST, preferred_element_type=F32
        )
        trail_left = pltpu.roll(mat[PIV:, :B], B - PIV, 1)
        trail_right = mat[PIV:, B:]
        mat[: B - PIV, :B] = trail_left - change[: B - PIV, :B]
        mat[: B - PIV, B:] = trail_right - change[: B - PIV, B:]

    lower = linv[...]
    own_t = jnp.dot(lower, rows_t, precision=HIGHEST, preferred_element_type=F32)
    lt[...] = jnp.dot(lower, at[...], precision=HIGHEST, preferred_element_type=F32)
    tr_v[...] = lt[:, pl.ds(pl.multiple_of(wide // 4 * B, B), B)].T
    panel_v[0] = tr_v[pl.ds(pl.multiple_of(wide % 4 * PIV, PIV), PIV), :]
    panel_out = pltpu.make_async_copy(panel_v, panel_hbm, out_sem.at[0])
    panel_out.start()
    update = lax.dot_general(
        own_t, lt[...], (((0,), (0,)), ((), ())), precision=HIGHEST, preferred_element_type=F32
    )

    @pl.loop(0, 16)
    def _(w):
        @pl.when(w != wide)
        def _():
            spread_from(w).wait_recv()

    row = iota((B, Q), 0)
    inside = (row // CYC % 4 == 0) & (wide * CYC + row % CYC < PIV)
    dropped = inside | (iota((B, Q), 1) < PIV)
    out_v[:, 0, :] = jnp.where(dropped, 0.0, f2r[...] - update)
    schur_out = pltpu.make_async_copy(out_v, schur_hbm, out_sem.at[1])
    schur_out.start()

    for n in range(2):
        exchange1(n).wait_send()
    for i in range(4):
        exchange2(i).wait_send()

    @pl.when(y == 0)
    def _():
        for j in range(1, 4):
            scatter(j).wait_send()

    for d in range(1, 4):
        along_z(d).wait_send()
        share(d).wait_send()
        for piece_z in range(4):
            along_y(piece_z, d).wait_send()

    @pl.loop(0, 16)
    def _(w):
        @pl.when(w != wide)
        def _():
            spread(w).wait_send()

    panel_out.wait()
    schur_out.wait()


def on_device(updates, entries1, entries2, leaf_maps, leaf_live, parent_maps, parent_live):
    operands = (updates, entries1, entries2, leaf_maps, leaf_live.T, parent_maps, parent_live)
    dma = pltpu.SemaphoreType.DMA
    vmem = pltpu.VMEM
    return pl.pallas_call(
        kernel,
        out_shape=(
            jax.ShapeDtypeStruct((1, PIV, B), F32),
            jax.ShapeDtypeStruct((B, 1, Q), F32),
        ),
        in_specs=[pl.BlockSpec(memory_space=pl.ANY)] * 7,
        out_specs=(pl.BlockSpec(memory_space=pl.ANY),) * 2,
        scratch_shapes=[
            vmem((B, 4 * Q), F32), vmem((B, 1, 2, Q), F32), vmem((B, 1, Q), F32),
            vmem((8, 4 * Q), jnp.int32), vmem((8, 4 * Q), jnp.int32),
            pltpu.SMEM((16, 32), jnp.int32), pltpu.SMEM((16, 16), jnp.int32),
            vmem((2, B, Q), F32), vmem((2, B, Q), F32), vmem((2, B, Q), F32),
            vmem((B, Q), F32), vmem((B, Q), F32), vmem((B, Q), F32), vmem((B, Q), F32),
            vmem((B, Q), F32), vmem((B, Q), F32), vmem((B, Q), F32),
            vmem((64, B), F32), vmem((4, 64, B), F32), vmem((B, 2 * B), F32), vmem((B, B), F32),
            vmem((B, B), F32), vmem((B, 1, Q), F32), vmem((1, PIV, B), F32),
            dma((7,)), dma((2,)), dma((2,)), dma((4,)), dma((4,)), dma((16,)), dma((16,)),
            dma((4,)), dma((1,)), dma((4,)), dma((4, 4)), dma((16,)), dma((4,)), dma((4,)), dma((2,)),
        ],
        compiler_params=pltpu.CompilerParams(
            collective_id=0, has_side_effects=True, vmem_limit_bytes=60 * 1024 * 1024
        ),
        cost_estimate=pl.CostEstimate(flops=600_000_000, bytes_accessed=3_000_000, transcendentals=0),
    )(*operands)


def solution(mesh):
    placed = (
        P("cube", "wide", None),
        P("wide", "cube", None, None),
        P("wide", "cube", None),
        P(),
        P(),
        P(),
        P(),
    )
    return jax.shard_map(
        on_device,
        mesh=mesh,
        in_specs=placed,
        out_specs=(P("cube", "wide", None), P("wide", "cube", None)),
        check_vma=False,
    )
```

time: 183 us -> 63.4 us (0.35); the launches traced: 180 us -> 63.2 us
  blocking collectives: 89 us -> 0 us
  Pallas kernels: 0 us -> 59.6 us
  other arithmetic: 28 us -> 0 us
  starting transfers between devices: 24.9 us -> 0 us
  waiting for transfers between devices: 19.2 us -> 0 us
  local copies, waits for them, and re-layouts: 12.7 us -> 2.99 us
  matrix products: 4.72 us -> 0 us
    all_gather x1 -> x0, blocking collectives: 61.8 us -> none  [on_device(): gathered = lax.all_gather(raw_panel, 'wide', axis=0, tiled=True)]
    pallas_call x0 -> x1, Pallas kernels: none -> 59.6 us  [on_device(): pl.pallas_call(kernel, out_shape=(jax.ShapeDtypeStruct((1, PIV, B), F32),...]
    all_to_all x1 -> x0, blocking collectives: 27.1 us -> none  [on_device(): lax.all_to_all(jnp.transpose(second_front.reshape(span_count, wide_count,...]
    ppermute x4 -> x0, starting transfers between devices: 24.9 us -> none  [from_partner(): lax.ppermute(array, axis, [(i, i ^ 1 << stride) for i in range(lax.axis_s...]
    another operation x6 -> x0, other arithmetic: 22.9 us -> none  [the longest x3 12.4 us: on_device(): pivot_block = jnp.linalg.cholesky(pivot_rows)]
    ppermute x4 -> x0, waiting for transfers between devices: 19.2 us -> none  [from_partner(): lax.ppermute(array, axis, [(i, i ^ 1 << stride) for i in range(lax.axis_s...]
    dot_general x6 -> x0, matrix products: 3.43 us -> none  [the longest x3 1.97 us: map_columns(): jnp.einsum('rhnj,hnjk->rhnk', mapped_rows, onehot_sel, precision=HIGHEST)]
    dynamic_slice x10 -> x0, local copies, waits for them, and re-layouts: 1.95 us -> none  [the longest x6 1.77 us: select_row(): return lax.dynamic_index_in_dim(lookup, position, 0, keepdims=False)]
  transfers between devices with their start and end apart: 4 -> 0, of which waited for: 4 -> 0; matrix products, arithmetic and copies ran while one was open for 2% -> 0% of each run, Pallas kernels for 0% -> 0%
where the time goes in v1:
time: 63.4 us; the launch traced here: 63.2 us
  Pallas kernels  59.6 us (94%)
  local copies, waits for them, and re-layouts  2.99 us (5%)
  between operations  0.64 us (1%)
    pallas_call x1, Pallas kernels, on_device(): pl.pallas_call(kernel, out_shape=(jax.ShapeDtypeStruct((1, PIV, B), F32),...  59.6 us
    unnamed x2, local copies, waits for them, and re-layouts  2.99 us

profile of v1, /device:TPU:1, one launch (start us, length us, event | category | flops | bytes accessed | tf_op | source)
XLA Modules:
  0.0 63.2 jit_solution(6954817127826912551)
XLA Ops:
  0.6 59.6 %shard_map.86 = (f32[1,32,128]{2,1,0:T(8,128)}, f32[128,1,512]{2,1,0:T(1,128)}) custom-call(f32[1,128,2048]{2,1,0:T(8,128)} %x_hbm.1, f32[128,1,2,512]{3,2,1,0:T(2,128)} %l1_hbm.1, f32[128,1,512]{2,1,0:T(1,128)} %l2_hbm.1, s32[32,2048]{1,0:T(8,128)} %lm_hbm.1, s32[16,32]{1,0:T(8,128)} %bitcast.1, s32[16,2048]{1,0:T(8,128)} %pm_hbm.1, s32[16,16]{1,0:T(8,128)} %pv_hbm.1), custom_call_target="tpu_custom_call" | custom-call | flops 600000000 | bytes 3000000 | tf_op jit(solution)/shard_map/pallas_call | solution.py:359
  60.2 1.3 %copy.11 = f32[1,32,128]{2,1,0:T(8,128)} copy(f32[1,32,128]{2,1,0:T(8,128)} %get-tuple-element.4) | data formatting | bytes 32768
  61.5 1.7 %copy.12 = f32[128,1,512]{2,1,0:T(1,128)} copy(f32[128,1,512]{2,1,0:T(1,128)} %get-tuple-element.5) | data formatting | bytes 524288

commit v2 on v1

--- a/solution.py
+++ b/solution.py
@@ -23,9 +23,10 @@
     x_hbm, l1_hbm, l2_hbm, lm_hbm, ll_hbm, pm_hbm, pv_hbm,
     panel_hbm, schur_hbm,
     x_v, l1_v, l2_v, lm_v, pm_v, ll_s, pv_s,
-    zs, zo, zr, us, uk, ur, f2, f2r, at, lt, msg, msgs, mat, linv, tr_v, out_v, panel_v,
+    zs, zo, zr, us, uk, ur, f2, f2r, at, lt, tiles, msgs, mat, linv, tr_v, out_v, panel_v,
     in_sem, e1_send, e1_recv, e2_send, e2_recv, aa_send, aa_recv,
-    sc_send, sc_recv, zg_send, yg_send, pg_recv, cb_send, cb_recv, out_sem,
+    sc_send, sc_recv, zg_send, yg_send, pg_recv, cb_send, cb_recv,
+    co_send, co_recv, cs_send, cs_recv, out_sem,
 ):
     cube = lax.axis_index("cube")
     wide = lax.axis_index("wide")
@@ -36,6 +37,7 @@
     z_hi = wide // 4
     y = wide % 4
     parent = cube // 2
+    lane = iota((B, B), 1)
 
     lm_base = pl.multiple_of(cube // 8 * 8, 8)
     pm_base = pl.multiple_of(parent // 8 * 8, 8)
@@ -191,8 +193,25 @@
             device_id=(cube, piece), device_id_type=MESH,
         )
 
+    def corner_to(w):
+        return pltpu.make_async_remote_copy(
+            src_ref=tiles.at[quarter, z_hi], dst_ref=tiles.at[quarter, z_hi],
+            send_sem=co_send.at[w], recv_sem=co_recv.at[z_hi],
+            device_id=(cube, w), device_id_type=MESH,
+        )
+
     @pl.when(y == 0)
     def _():
+        tile = f2[:CYC, :B]
+        for r in range(1, 4):
+            moved = pltpu.roll(f2[CYC * r : CYC * (r + 1), :B], PIV * r, 1)
+            tile = jnp.where(lane[:CYC] >= PIV * r, moved, tile)
+        tiles[quarter, z_hi] = tile
+
+        @pl.loop(0, 15)
+        def _(n):
+            corner_to((wide + 8 + n + (n >= 8)) % 16).start()
+
         for j in range(1, 4):
             scatter(j).start()
         at[rows_of(wide), :] = f2[:CYC, :]
@@ -210,7 +229,31 @@
     for d in (2, 1, 3):
         along_y(z_hi, d).start()
 
+    def share_corner(d):
+        return pltpu.make_async_remote_copy(
+            src_ref=tiles.at[quarter], dst_ref=tiles.at[quarter],
+            send_sem=cs_send.at[d], recv_sem=cs_recv.at[quarter],
+            device_id=(cube ^ d, wide), device_id_type=MESH,
+        )
+
+    def corner_from(q):
+        return pltpu.make_async_remote_copy(
+            src_ref=tiles.at[quarter, q], dst_ref=tiles.at[quarter, q],
+            send_sem=co_send.at[0], recv_sem=co_recv.at[q],
+            device_id=(cube, 4 * q), device_id_type=MESH,
+        )
+
     for o in order:
+        if o == 3:
+            for q in range(4):
+
+                @pl.when(wide != 4 * q)
+                def _():
+                    corner_from(q).wait_recv()
+
+            for d in (2, 3, 1):
+                share_corner(d).start()
+
         chunk = (z_hi + o) % 4
 
         @pl.when(chunk != 0)
@@ -232,83 +275,105 @@
         for d in (2, 1, 3):
             along_y(piece_z, d).start()
 
-    @pl.loop(0, 16)
-    def _(piece):
-        @pl.when(piece % 4 != y)
-        def _():
-            piece_from(piece).wait_recv()
-
-    lane = iota((B, B), 1)
-    packed = at[:, :B]
-    for i in range(4):
-        shift = (PIV + CYC * i - CYC * wide + B) % B
-        moved = pltpu.roll(at[:, i * B : (i + 1) * B], shift, 1)
-        packed = jnp.where((lane >= PIV + CYC * i) & (lane < PIV + CYC * (i + 1)), moved, packed)
-    msg[...] = jnp.where(lane[:64] < 64, packed[:64], pltpu.roll(packed[64:], 64, 1))
-
-    def share(d):
-        return pltpu.make_async_remote_copy(
-            src_ref=msg, dst_ref=msgs.at[quarter], send_sem=cb_send.at[d], recv_sem=cb_recv.at[quarter],
-            device_id=(cube ^ d, wide), device_id_type=MESH,
-        )
-
-    for d in range(1, 4):
-        share(d).start()
-    msgs[quarter] = msg[...]
-
     for d in range(1, 4):
         other = quarter ^ d
         pltpu.make_async_remote_copy(
-            src_ref=msg, dst_ref=msgs.at[other], send_sem=cb_send.at[d], recv_sem=cb_recv.at[other],
+            src_ref=tiles.at[other], dst_ref=tiles.at[other],
+            send_sem=cs_send.at[d], recv_sem=cs_recv.at[other],
             device_id=(group + other, wide), device_id_type=MESH,
         ).wait_recv()
 
-    def unpack(first_lane):
-        got = jnp.zeros((64, B), F32)
-        for i in range(4):
-            moved = pltpu.roll(msgs[i], (PIV * i - first_lane) % B, 1)
-            got = jnp.where((lane[:64] >= PIV * i) & (lane[:64] < PIV * (i + 1)), moved, got)
+    def gathered(parts, r):
+        got = parts[0]
+        if r:
+            got = pltpu.roll(got, B - PIV * r, 1)
+        for c in range(1, 4):
+            moved = parts[c] if c == r else pltpu.roll(parts[c], PIV * (c - r) % B, 1)
+            got = jnp.where(lane[:PIV] >= PIV * c, moved, got)
         return got
 
-    mat[:64, :B] = unpack(0)
-    mat[64:, :B] = unpack(64)
-    rows_t = jnp.concatenate((unpack(32), unpack(96)), axis=0)
+    corners = [tiles[c].reshape(PIV, B) for c in range(4)]
+    for r in range(4):
+        got = gathered(corners, r)
+        for q in range(4):
+            mat[PIV * q + CYC * r : PIV * q + CYC * (r + 1), :B] = got[CYC * q : CYC * (q + 1)]
     mat[:, B:] = jnp.where(iota((B, B), 0) == lane, 1.0, 0.0)
+
+    def share(d):
+        return pltpu.make_async_remote_copy(
+            src_ref=msgs.at[quarter], dst_ref=msgs.at[quarter],
+            send_sem=cb_send.at[d], recv_sem=cb_recv.at[quarter],
+            device_id=(cube ^ d, wide), device_id_type=MESH,
+        )
 
     @pl.loop(0, 4)
     def _(step):
+        @pl.when(step == 2)
+        def _():
+            @pl.loop(0, 16)
+            def _(piece):
+                @pl.when(piece % 4 != y)
+                def _():
+                    piece_from(piece).wait_recv()
+
+            packed = jnp.zeros((PIV, B), F32)
+            for r in range(4):
+                for i in range(4):
+                    first = PIV * r + CYC * i
+                    part = at[PIV * r : PIV * (r + 1), B * i : B * (i + 1)]
+                    moved = pltpu.roll(part, (first + B - CYC * wide) % B, 1)
+                    packed = jnp.where(lane[:PIV] >= first, moved, packed)
+            msgs[quarter] = packed
+            for d in (2, 3, 1):
+                share(d).start()
+
         left = mat[:PIV, :B]
         right = mat[:PIV, B:]
-        row_id = iota((PIV, 1), 0)
-        diag = jnp.ones((PIV, 1), F32)
-        for j in range(PIV):
-            pivot = left[j : j + 1, j : j + 1]
-            column = left[:, j : j + 1]
-            diag = jnp.where(row_id == j, pivot, diag)
-            factor = jnp.where(row_id > j, column * (1.0 / pivot), 0.0)
-            left = left - factor * left[j : j + 1, :]
-            right = right - factor * right[j : j + 1, :]
+        row_id = iota((PIV, B), 0)
+        diag = jnp.ones((PIV, B), F32)
+        for first in range(0, PIV, CYC):
+            columns = [jnp.broadcast_to(left[:, first + n : first + n + 1], (PIV, B)) for n in range(CYC)]
+            for n in range(CYC):
+                j = first + n
+                pivot = columns[n][j : j + 1, :]
+                diag = jnp.where(row_id == j, pivot, diag)
+                factor = jnp.where(row_id > j, columns[n] * (1.0 / pivot), 0.0)
+                for m in range(n + 1, CYC):
+                    columns[m] = columns[m] - factor * columns[m][j : j + 1, :]
+                left = left - factor * left[j : j + 1, :]
+                right = right - factor * right[j : j + 1, :]
         scale = lax.rsqrt(diag)
-        left = pltpu.roll(left * scale, B - PIV, 1)
-        left = jnp.where(lane[:PIV] < B - PIV, left, 0.0)
         right = right * scale
         linv[pl.ds(pl.multiple_of(step * PIV, PIV), PIV), :] = right
-        both = jnp.concatenate((left, right), axis=1)
-        change = lax.dot_general(
-            left, both, (((0,), (0,)), ((), ())), precision=HIGHEST, preferred_element_type=F32
-        )
-        trail_left = pltpu.roll(mat[PIV:, :B], B - PIV, 1)
-        trail_right = mat[PIV:, B:]
-        mat[: B - PIV, :B] = trail_left - change[: B - PIV, :B]
-        mat[: B - PIV, B:] = trail_right - change[: B - PIV, B:]
+
+        @pl.when(step < 3)
+        def _():
+            moved = pltpu.roll(left * scale, B - PIV, 1)
+            moved = jnp.where(lane[:PIV] < B - PIV, moved, 0.0)
+            both = jnp.concatenate((moved, right), axis=1)
+            change = lax.dot_general(
+                moved, both, (((0,), (0,)), ((), ())), precision=HIGHEST, preferred_element_type=F32
+            )
+            trail_left = pltpu.roll(mat[PIV:, :B], B - PIV, 1)
+            trail_right = mat[PIV:, B:]
+            mat[: B - PIV, :B] = trail_left - change[: B - PIV, :B]
+            mat[: B - PIV, B:] = trail_right - change[: B - PIV, B:]
 
     lower = linv[...]
-    own_t = jnp.dot(lower, rows_t, precision=HIGHEST, preferred_element_type=F32)
     lt[...] = jnp.dot(lower, at[...], precision=HIGHEST, preferred_element_type=F32)
     tr_v[...] = lt[:, pl.ds(pl.multiple_of(wide // 4 * B, B), B)].T
-    panel_v[0] = tr_v[pl.ds(pl.multiple_of(wide % 4 * PIV, PIV), PIV), :]
-    panel_out = pltpu.make_async_copy(panel_v, panel_hbm, out_sem.at[0])
-    panel_out.start()
+    panel_hbm[0] = tr_v[pl.ds(pl.multiple_of(wide % 4 * PIV, PIV), PIV), :]
+    for d in range(1, 4):
+        other = quarter ^ d
+        pltpu.make_async_remote_copy(
+            src_ref=msgs.at[other], dst_ref=msgs.at[other],
+            send_sem=cb_send.at[d], recv_sem=cb_recv.at[other],
+            device_id=(group + other, wide), device_id_type=MESH,
+        ).wait_recv()
+
+    shared = [msgs[c] for c in range(4)]
+    rows_t = jnp.concatenate([gathered(shared, r) for r in range(4)], axis=0)
+    own_t = jnp.dot(lower, rows_t, precision=HIGHEST, preferred_element_type=F32)
     update = lax.dot_general(
         own_t, lt[...], (((0,), (0,)), ((), ())), precision=HIGHEST, preferred_element_type=F32
     )
@@ -322,9 +387,7 @@
     row = iota((B, Q), 0)
     inside = (row // CYC % 4 == 0) & (wide * CYC + row % CYC < PIV)
     dropped = inside | (iota((B, Q), 1) < PIV)
-    out_v[:, 0, :] = jnp.where(dropped, 0.0, f2r[...] - update)
-    schur_out = pltpu.make_async_copy(out_v, schur_hbm, out_sem.at[1])
-    schur_out.start()
+    schur_hbm[:, 0, :] = jnp.where(dropped, 0.0, f2r[...] - update)
 
     for n in range(2):
         exchange1(n).wait_send()
@@ -336,9 +399,14 @@
         for j in range(1, 4):
             scatter(j).wait_send()
 
+        @pl.loop(1, 16)
+        def _(d):
+            corner_to((wide + d) % 16).wait_send()
+
     for d in range(1, 4):
         along_z(d).wait_send()
         share(d).wait_send()
+        share_corner(d).wait_send()
         for piece_z in range(4):
             along_y(piece_z, d).wait_send()
 
@@ -348,12 +416,10 @@
         def _():
             spread(w).wait_send()
 
-    panel_out.wait()
-    schur_out.wait()
-
 
 def on_device(updates, entries1, entries2, leaf_maps, leaf_live, parent_maps, parent_live):
     operands = (updates, entries1, entries2, leaf_maps, leaf_live.T, parent_maps, parent_live)
+    operands = tuple(pltpu.with_memory_space_constraint(o, pltpu.HBM) for o in operands)
     dma = pltpu.SemaphoreType.DMA
     vmem = pltpu.VMEM
     return pl.pallas_call(
@@ -362,8 +428,8 @@
             jax.ShapeDtypeStruct((1, PIV, B), F32),
             jax.ShapeDtypeStruct((B, 1, Q), F32),
         ),
-        in_specs=[pl.BlockSpec(memory_space=pl.ANY)] * 7,
-        out_specs=(pl.BlockSpec(memory_space=pl.ANY),) * 2,
+        in_specs=[pl.BlockSpec(memory_space=pltpu.HBM)] * 7,
+        out_specs=(pl.BlockSpec(memory_space=pltpu.VMEM),) * 2,
         scratch_shapes=[
             vmem((B, 4 * Q), F32), vmem((B, 1, 2, Q), F32), vmem((B, 1, Q), F32),
             vmem((8, 4 * Q), jnp.int32), vmem((8, 4 * Q), jnp.int32),
@@ -371,13 +437,14 @@
             vmem((2, B, Q), F32), vmem((2, B, Q), F32), vmem((2, B, Q), F32),
             vmem((B, Q), F32), vmem((B, Q), F32), vmem((B, Q), F32), vmem((B, Q), F32),
             vmem((B, Q), F32), vmem((B, Q), F32), vmem((B, Q), F32),
-            vmem((64, B), F32), vmem((4, 64, B), F32), vmem((B, 2 * B), F32), vmem((B, B), F32),
+            vmem((4, 4, CYC, B), F32), vmem((4, PIV, B), F32), vmem((B, 2 * B), F32), vmem((B, B), F32),
             vmem((B, B), F32), vmem((B, 1, Q), F32), vmem((1, PIV, B), F32),
             dma((7,)), dma((2,)), dma((2,)), dma((4,)), dma((4,)), dma((16,)), dma((16,)),
-            dma((4,)), dma((1,)), dma((4,)), dma((4, 4)), dma((16,)), dma((4,)), dma((4,)), dma((2,)),
+            dma((4,)), dma((1,)), dma((4,)), dma((4, 4)), dma((16,)), dma((4,)), dma((4,)),
+            dma((16,)), dma((4,)), dma((4,)), dma((4,)), dma((2,)),
         ],
         compiler_params=pltpu.CompilerParams(
-            collective_id=0, has_side_effects=True, vmem_limit_bytes=60 * 1024 * 1024
+            collective_id=0, has_side_effects=True, vmem_limit_bytes=16 * 1024 * 1024
         ),
         cost_estimate=pl.CostEstimate(flops=600_000_000, bytes_accessed=3_000_000, transcendentals=0),
     )(*operands)

time: 63.4 us -> 55.3 us (0.87)
  Pallas kernels: 59.6 us -> 53.2 us
  local copies, waits for them, and re-layouts: 2.99 us -> 1.31 us
    pallas_call x1, Pallas kernels: 59.6 us -> 53.2 us  [on_device(): pl.pallas_call(kernel, out_shape=(jax.ShapeDtypeStruct((1, PIV, B), F32),...]
    unnamed x2, local copies, waits for them, and re-layouts: 2.99 us -> 1.31 us
where the time goes in v2:
time: 55.3 us; the launch traced here: 55.1 us
  Pallas kernels  53.2 us (96%)
  local copies, waits for them, and re-layouts  1.31 us (2%)
  between operations  0.64 us (1%)
    pallas_call x1, Pallas kernels, on_device(): pl.pallas_call(kernel, out_shape=(jax.ShapeDtypeStruct((1, PIV, B), F32),...  53.2 us
    unnamed x2, local copies, waits for them, and re-layouts  1.31 us

profile of v2, /device:TPU:1, one launch (start us, length us, event | category | flops | bytes accessed | tf_op | source)
XLA Modules:
  0.0 55.1 jit_solution(1711058933456357873)
XLA Ops:
  0.6 53.2 %shard_map.86 = (f32[1,32,128]{2,1,0:T(8,128)S(1)}, f32[128,1,512]{2,1,0:T(1,128)S(1)}) custom-call(f32[1,128,2048]{2,1,0:T(8,128)} %x_hbm.1, f32[128,1,2,512]{3,2,1,0:T(2,128)} %l1_hbm.1, f32[128,1,512]{2,1,0:T(1,128)} %l2_hbm.1, s32[32,2048]{1,0:T(8,128)} %lm_hbm.1, s32[16,32]{1,0:T(8,128)} %bitcast.1, s32[16,2048]{1,0:T(8,128)} %pm_hbm.1, s32[16,16]{1,0:T(8,128)} %pv_hbm.1), custom_call_target="tpu_custom_call" | custom-call | flops 600000000 | bytes 3000000 | tf_op jit(solution)/shard_map/pallas_call | solution.py:425
  53.8 0.6 %copy.11 = f32[1,32,128]{2,1,0:T(8,128)} copy(f32[1,32,128]{2,1,0:T(8,128)S(1)} %get-tuple-element.4) | data formatting | bytes 32768
  54.4 0.7 %copy.12 = f32[128,1,512]{2,1,0:T(1,128)} copy(f32[128,1,512]{2,1,0:T(1,128)S(1)} %get-tuple-element.5) | data formatting | bytes 524288

commit v3 on v2

--- a/solution.py
+++ b/solution.py
@@ -23,10 +23,10 @@
     x_hbm, l1_hbm, l2_hbm, lm_hbm, ll_hbm, pm_hbm, pv_hbm,
     panel_hbm, schur_hbm,
     x_v, l1_v, l2_v, lm_v, pm_v, ll_s, pv_s,
-    zs, zo, zr, us, uk, ur, f2, f2r, at, lt, tiles, msgs, mat, linv, tr_v, out_v, panel_v,
-    in_sem, e1_send, e1_recv, e2_send, e2_recv, aa_send, aa_recv,
-    sc_send, sc_recv, zg_send, yg_send, pg_recv, cb_send, cb_recv,
-    co_send, co_recv, cs_send, cs_recv, out_sem,
+    zs, zo, zr, us, uk, ur, f2, f2r, tt, at, lt, cr, terms, tiles, msgs, mat, linv, tr_v,
+    in_sem, e1_send, e1_recv, e2_send, e2_recv, aa_send, aa_recv, ac_send,
+    cr_send, cr_recv, pa_send, pb_send, pa_recv, zg_send, yg_send, pg_recv, cb_send, cb_recv,
+    co_send, co_recv, cs_send, cs_recv,
 ):
     cube = lax.axis_index("cube")
     wide = lax.axis_index("wide")
@@ -38,6 +38,13 @@
     y = wide % 4
     parent = cube // 2
     lane = iota((B, B), 1)
+
+    def ring(a, b):
+        m = (a - b + 4) % 4
+        return m - m // 3 * 2
+
+    def by_rows(part, home, at_z):
+        return ring(part, at_z) <= ring(home, at_z)
 
     lm_base = pl.multiple_of(cube // 8 * 8, 8)
     pm_base = pl.multiple_of(parent // 8 * 8, 8)
@@ -54,12 +61,26 @@
         load.start()
 
     barrier = pltpu.get_barrier_semaphore()
-    for d in range(1, 4):
-        pl.semaphore_signal(barrier, inc=1, device_id=(cube ^ d, wide), device_id_type=MESH)
-
-    @pl.loop(1, 16)
-    def _(d):
-        pl.semaphore_signal(barrier, inc=1, device_id=(cube, (wide + d) % 16), device_id_type=MESH)
+
+    def greet(c, w):
+        pl.semaphore_signal(barrier, inc=1, device_id=(c, w), device_id_type=MESH)
+
+    @pl.loop(0, 15)
+    def _(n):
+        greet(cube, (wide + 8 + n + n // 8) % 16)
+
+    for part in range(4):
+
+        @pl.when(jnp.logical_not(by_rows(part, quarter, z_hi)))
+        def _():
+            for k in range(4):
+                greet(group + part, 4 * quarter + k)
+
+    greet(cube ^ 2, 4 * z_hi)
+    for d in (2, 3, 1):
+        greet(cube ^ d, wide)
+    apart = ring(z_hi, quarter)
+    greetings = 18 + 4 * (apart % 2 * 2 + apart // 2) + 4 * (1 - (y + 3) // 4)
 
     def one_hot(map_ref, live_ref, live_row, block):
         lanes = pl.multiple_of(block * B, B)
@@ -101,7 +122,7 @@
         half = 1 - high if n == 0 else high
         zs[n] = leaf_quarter(2 * half + 1 - low)
         if n == 0:
-            pl.semaphore_wait(barrier, 18)
+            pl.semaphore_wait(barrier, greetings)
         exchange1(n).start()
     for n in range(2):
         half = 1 - high if n == 0 else high
@@ -128,47 +149,45 @@
 
     exchange1(0).wait_recv()
     us[...] = upper_quarter(0)
-    exchange2(0).start()
+    def rows_of(w):
+        return pl.ds(pl.multiple_of(w * CYC, CYC), CYC)
+
+    def corner_term():
+        return pltpu.make_async_remote_copy(
+            src_ref=us.at[pl.ds(0, PIV), pl.ds(0, B)], dst_ref=cr, send_sem=cr_send, recv_sem=cr_recv,
+            device_id=(cube ^ 2, wide), device_id_type=MESH,
+        )
+
+    def pivot_term(j):
+        return pltpu.make_async_remote_copy(
+            src_ref=us.at[pl.ds(j * CYC, CYC)], dst_ref=terms.at[0], send_sem=pa_send.at[j], recv_sem=pa_recv.at[0],
+            device_id=(cube ^ 2, 4 * z_hi + j), device_id_type=MESH,
+        )
+
+    def own_term(j):
+        return pltpu.make_async_remote_copy(
+            src_ref=uk.at[pl.ds(j * CYC, CYC)], dst_ref=terms.at[1], send_sem=pb_send.at[j], recv_sem=pa_recv.at[1],
+            device_id=(cube, 4 * z_hi + j), device_id_type=MESH,
+        )
+
+    @pl.when(y == 0)
+    def _():
+        corner_term().start()
+        for j in (2, 1, 3, 0):
+            pivot_term(j).start()
+
     order = (2, 1, 3, 0)
     for o in order:
-        chunk = (z_hi + o) % 4
-
-        @pl.when(chunk != 0)
-        def _():
-            exchange2(chunk).start()
+        exchange2((z_hi + o) % 4).start()
 
     exchange1(1).wait_recv()
     uk[...] = upper_quarter(1) + l2_v[:, 0, :]
 
-    def finish_chunk(i):
-        exchange2(i).wait_recv()
-        rows = pl.ds(pl.multiple_of(i * 32, 32), 32)
-        f2[rows, :] = uk[rows, :] + ur[rows, :]
-
-    def rows_of(w):
-        return pl.ds(pl.multiple_of(w * CYC, CYC), CYC)
-
-    def spread(w):
-        return pltpu.make_async_remote_copy(
-            src_ref=f2.at[rows_of(w)], dst_ref=f2r.at[rows_of(wide)],
-            send_sem=aa_send.at[w], recv_sem=aa_recv.at[wide],
+    def corner_to(w):
+        return pltpu.make_async_remote_copy(
+            src_ref=tiles.at[quarter, z_hi], dst_ref=tiles.at[quarter, z_hi],
+            send_sem=co_send.at[w], recv_sem=co_recv.at[z_hi],
             device_id=(cube, w), device_id_type=MESH,
-        )
-
-    def spread_from(w):
-        return pltpu.make_async_remote_copy(
-            src_ref=f2.at[rows_of(w)], dst_ref=f2r.at[rows_of(w)],
-            send_sem=aa_send.at[w], recv_sem=aa_recv.at[w],
-            device_id=(cube, w), device_id_type=MESH,
-        )
-
-    finish_chunk(0)
-
-    def scatter(j):
-        return pltpu.make_async_remote_copy(
-            src_ref=f2.at[pl.ds(j * CYC, CYC)], dst_ref=at.at[rows_of(4 * z_hi + j)],
-            send_sem=sc_send.at[j], recv_sem=sc_recv.at[0],
-            device_id=(cube, 4 * z_hi + j), device_id_type=MESH,
         )
 
     def along_z(d):
@@ -193,36 +212,36 @@
             device_id=(cube, piece), device_id_type=MESH,
         )
 
-    def corner_to(w):
-        return pltpu.make_async_remote_copy(
-            src_ref=tiles.at[quarter, z_hi], dst_ref=tiles.at[quarter, z_hi],
-            send_sem=co_send.at[w], recv_sem=co_recv.at[z_hi],
-            device_id=(cube, w), device_id_type=MESH,
+    def term_from(n):
+        return pltpu.make_async_remote_copy(
+            src_ref=us.at[pl.ds(0, CYC)], dst_ref=terms.at[n], send_sem=pa_send.at[0], recv_sem=pa_recv.at[n],
+            device_id=(cube ^ 2, 4 * z_hi), device_id_type=MESH,
         )
 
     @pl.when(y == 0)
     def _():
-        tile = f2[:CYC, :B]
+        for j in (2, 1, 3):
+            own_term(j).start()
+        corner_term().wait_recv()
+        block = uk[:PIV, :B] + cr[...]
+        tile = block[:CYC]
         for r in range(1, 4):
-            moved = pltpu.roll(f2[CYC * r : CYC * (r + 1), :B], PIV * r, 1)
+            moved = pltpu.roll(block[CYC * r : CYC * (r + 1)], PIV * r, 1)
             tile = jnp.where(lane[:CYC] >= PIV * r, moved, tile)
         tiles[quarter, z_hi] = tile
 
         @pl.loop(0, 15)
         def _(n):
-            corner_to((wide + 8 + n + (n >= 8)) % 16).start()
-
-        for j in range(1, 4):
-            scatter(j).start()
-        at[rows_of(wide), :] = f2[:CYC, :]
+            corner_to((wide + 8 + n + n // 8) % 16).start()
+
+        term_from(0).wait_recv()
+        at[rows_of(wide), :] = terms[0] + uk[:CYC, :]
 
     @pl.when(y != 0)
     def _():
-        pltpu.make_async_remote_copy(
-            src_ref=f2.at[pl.ds(0, CYC)], dst_ref=at.at[rows_of(wide)],
-            send_sem=sc_send.at[0], recv_sem=sc_recv.at[0],
-            device_id=(cube, 4 * z_hi), device_id_type=MESH,
-        ).wait_recv()
+        term_from(0).wait_recv()
+        term_from(1).wait_recv()
+        at[rows_of(wide), :] = terms[0] + terms[1]
 
     for d in (2, 1, 3):
         along_z(d).start()
@@ -243,31 +262,85 @@
             device_id=(cube, 4 * q), device_id_type=MESH,
         )
 
+    def spread_rows(w):
+        return pltpu.make_async_remote_copy(
+            src_ref=f2.at[rows_of(w)], dst_ref=f2r.at[z_hi, y],
+            send_sem=aa_send.at[w], recv_sem=aa_recv.at[wide],
+            device_id=(cube, w), device_id_type=MESH,
+        )
+
+    def spread_columns(w):
+        return pltpu.make_async_remote_copy(
+            src_ref=tt.at[:, w], dst_ref=f2r.at[quarter, :, :, pl.ds(pl.multiple_of(y * B, B), B)],
+            send_sem=ac_send.at[w], recv_sem=aa_recv.at[4 * quarter + y],
+            device_id=(group + z_hi, w), device_id_type=MESH,
+        )
+
+    def rows_from(part, k):
+        return pltpu.make_async_remote_copy(
+            src_ref=f2.at[rows_of(0)], dst_ref=f2r.at[part, k],
+            send_sem=aa_send.at[0], recv_sem=aa_recv.at[4 * part + k],
+            device_id=(cube, 4 * part + k), device_id_type=MESH,
+        )
+
+    def columns_from(part, k):
+        return pltpu.make_async_remote_copy(
+            src_ref=tt.at[:, 0], dst_ref=f2r.at[part, :, :, pl.ds(k * B, B)],
+            send_sem=ac_send.at[0], recv_sem=aa_recv.at[4 * part + k],
+            device_id=(group + part, 4 * quarter + k), device_id_type=MESH,
+        )
+
     for o in order:
-        if o == 3:
-            for q in range(4):
-
-                @pl.when(wide != 4 * q)
+        chunk = (z_hi + o) % 4
+        exchange2(chunk).wait_recv()
+        rows = pl.ds(pl.multiple_of(chunk * 32, 32), 32)
+        f2[rows, :] = uk[rows, :] + ur[rows, :]
+
+        @pl.when(by_rows(z_hi, quarter, chunk))
+        def _():
+            for k in range(4):
+                w = 4 * chunk + k
+
+                @pl.when(w != wide)
                 def _():
-                    corner_from(q).wait_recv()
-
-            for d in (2, 3, 1):
-                share_corner(d).start()
-
-        chunk = (z_hi + o) % 4
-
-        @pl.when(chunk != 0)
-        def _():
-            finish_chunk(chunk)
-
-        for k in range(4):
-            w = 4 * chunk + k
-
-            @pl.when(w != wide)
+                    spread_rows(w).start()
+
+    f2r[z_hi, y] = f2[rows_of(wide), :]
+
+    @pl.when(z_hi != quarter)
+    def _():
+        for i in range(4):
+            tt[i] = f2[:, i * B : (i + 1) * B].T.reshape(16, CYC, B)
+        for o in (1, 3, 0):
+            chunk = (z_hi + o) % 4
+
+            @pl.when(ring(z_hi, chunk) < ring(quarter, chunk))
             def _():
-                spread(w).start()
-
-    f2r[rows_of(wide), :] = f2[rows_of(wide), :]
+                for k in range(4):
+                    spread_columns(4 * chunk + k).start()
+
+    def share_corner(d):
+        return pltpu.make_async_remote_copy(
+            src_ref=tiles.at[quarter], dst_ref=tiles.at[quarter],
+            send_sem=cs_send.at[d], recv_sem=cs_recv.at[quarter],
+            device_id=(cube ^ d, wide), device_id_type=MESH,
+        )
+
+    def corner_from(q):
+        return pltpu.make_async_remote_copy(
+            src_ref=tiles.at[quarter, q], dst_ref=tiles.at[quarter, q],
+            send_sem=co_send.at[0], recv_sem=co_recv.at[q],
+            device_id=(cube, 4 * q), device_id_type=MESH,
+        )
+
+    for q in range(4):
+
+        @pl.when(wide != 4 * q)
+        def _():
+            corner_from(q).wait_recv()
+
+    for d in (2, 3, 1):
+        share_corner(d).start()
 
     for o in (1, 3, 2):
         piece_z = (z_hi + o) % 4
@@ -378,16 +451,22 @@
         own_t, lt[...], (((0,), (0,)), ((), ())), precision=HIGHEST, preferred_element_type=F32
     )
 
-    @pl.loop(0, 16)
-    def _(w):
-        @pl.when(w != wide)
-        def _():
-            spread_from(w).wait_recv()
+    for part in range(4):
+        as_rows = by_rows(part, quarter, z_hi)
+        for k in range(4):
+
+            @pl.when(as_rows & (wide != 4 * part + k))
+            def _():
+                rows_from(part, k).wait_recv()
+
+            @pl.when(jnp.logical_not(as_rows))
+            def _():
+                columns_from(part, k).wait_recv()
 
     row = iota((B, Q), 0)
     inside = (row // CYC % 4 == 0) & (wide * CYC + row % CYC < PIV)
     dropped = inside | (iota((B, Q), 1) < PIV)
-    schur_hbm[:, 0, :] = jnp.where(dropped, 0.0, f2r[...] - update)
+    schur_hbm[:, 0, :] = jnp.where(dropped, 0.0, f2r[...].reshape(B, Q) - update)
 
     for n in range(2):
         exchange1(n).wait_send()
@@ -396,8 +475,11 @@
 
     @pl.when(y == 0)
     def _():
+        corner_term().wait_send()
+        for j in range(4):
+            pivot_term(j).wait_send()
         for j in range(1, 4):
-            scatter(j).wait_send()
+            own_term(j).wait_send()
 
         @pl.loop(1, 16)
         def _(d):
@@ -410,11 +492,22 @@
         for piece_z in range(4):
             along_y(piece_z, d).wait_send()
 
-    @pl.loop(0, 16)
-    def _(w):
-        @pl.when(w != wide)
-        def _():
-            spread(w).wait_send()
+    for o in range(4):
+        chunk = (z_hi + o) % 4
+
+        @pl.when(by_rows(z_hi, quarter, chunk))
+        def _():
+            for k in range(4):
+                w = 4 * chunk + k
+
+                @pl.when(w != wide)
+                def _():
+                    spread_rows(w).wait_send()
+
+        @pl.when(ring(z_hi, chunk) < ring(quarter, chunk))
+        def _():
+            for k in range(4):
+                spread_columns(4 * chunk + k).wait_send()
 
 
 def on_device(updates, entries1, entries2, leaf_maps, leaf_live, parent_maps, parent_live):
@@ -436,12 +529,13 @@
             pltpu.SMEM((16, 32), jnp.int32), pltpu.SMEM((16, 16), jnp.int32),
             vmem((2, B, Q), F32), vmem((2, B, Q), F32), vmem((2, B, Q), F32),
             vmem((B, Q), F32), vmem((B, Q), F32), vmem((B, Q), F32), vmem((B, Q), F32),
-            vmem((B, Q), F32), vmem((B, Q), F32), vmem((B, Q), F32),
+            vmem((4, 4, CYC, Q), F32), vmem((4, 16, CYC, B), F32), vmem((B, Q), F32), vmem((B, Q), F32),
+            vmem((PIV, B), F32), vmem((2, CYC, Q), F32),
             vmem((4, 4, CYC, B), F32), vmem((4, PIV, B), F32), vmem((B, 2 * B), F32), vmem((B, B), F32),
-            vmem((B, B), F32), vmem((B, 1, Q), F32), vmem((1, PIV, B), F32),
-            dma((7,)), dma((2,)), dma((2,)), dma((4,)), dma((4,)), dma((16,)), dma((16,)),
-            dma((4,)), dma((1,)), dma((4,)), dma((4, 4)), dma((16,)), dma((4,)), dma((4,)),
-            dma((16,)), dma((4,)), dma((4,)), dma((4,)), dma((2,)),
+            vmem((B, B), F32),
+            dma((7,)), dma((2,)), dma((2,)), dma((4,)), dma((4,)), dma((16,)), dma((16,)), dma((16,)),
+            dma, dma, dma((4,)), dma((4,)), dma((2,)), dma((4,)), dma((4, 4)), dma((16,)), dma((4,)), dma((4,)),
+            dma((16,)), dma((4,)), dma((4,)), dma((4,)),
         ],
         compiler_params=pltpu.CompilerParams(
             collective_id=0, has_side_effects=True, vmem_limit_bytes=16 * 1024 * 1024

time: 55.3 us -> 52.4 us (0.948)
  Pallas kernels: 53.2 us -> 50.3 us
    pallas_call x1, Pallas kernels: 53.2 us -> 50.3 us  [on_device(): pl.pallas_call(kernel, out_shape=(jax.ShapeDtypeStruct((1, PIV, B), F32),...]
where the time goes in v3:
time: 52.4 us; the launch traced here: 52.3 us
  Pallas kernels  50.3 us (96%)
  local copies, waits for them, and re-layouts  1.31 us (2%)
  between operations  0.64 us (1%)
    pallas_call x1, Pallas kernels, on_device(): pl.pallas_call(kernel, out_shape=(jax.ShapeDtypeStruct((1, PIV, B), F32),...  50.3 us
    unnamed x2, local copies, waits for them, and re-layouts  1.31 us

profile of v3, /device:TPU:1, one launch (start us, length us, event | category | flops | bytes accessed | tf_op | source)
XLA Modules:
  0.0 52.3 jit_solution(12304231666619770935)
XLA Ops:
  0.6 50.3 %shard_map.86 = (f32[1,32,128]{2,1,0:T(8,128)S(1)}, f32[128,1,512]{2,1,0:T(1,128)S(1)}) custom-call(f32[1,128,2048]{2,1,0:T(8,128)} %x_hbm.1, f32[128,1,2,512]{3,2,1,0:T(2,128)} %l1_hbm.1, f32[128,1,512]{2,1,0:T(1,128)} %l2_hbm.1, s32[32,2048]{1,0:T(8,128)} %lm_hbm.1, s32[16,32]{1,0:T(8,128)} %bitcast.1, s32[16,2048]{1,0:T(8,128)} %pm_hbm.1, s32[16,16]{1,0:T(8,128)} %pv_hbm.1), custom_call_target="tpu_custom_call" | custom-call | flops 600000000 | bytes 3000000 | tf_op jit(solution)/shard_map/pallas_call | solution.py:518
  50.9 0.6 %copy.11 = f32[1,32,128]{2,1,0:T(8,128)} copy(f32[1,32,128]{2,1,0:T(8,128)S(1)} %get-tuple-element.4) | data formatting | bytes 32768
  51.5 0.7 %copy.12 = f32[128,1,512]{2,1,0:T(1,128)} copy(f32[128,1,512]{2,1,0:T(1,128)S(1)} %get-tuple-element.5) | data formatting | bytes 524288

commit v4 on v3

--- a/solution.py
+++ b/solution.py
@@ -177,8 +177,11 @@
             pivot_term(j).start()
 
     order = (2, 1, 3, 0)
-    for o in order:
-        exchange2((z_hi + o) % 4).start()
+    exchange2((z_hi + 2) % 4).start()
+
+    @pl.when(y != 0)
+    def _():
+        exchange2((z_hi + 1) % 4).start()
 
     exchange1(1).wait_recv()
     uk[...] = upper_quarter(1) + l2_v[:, 0, :]
@@ -248,6 +251,13 @@
     for d in (2, 1, 3):
         along_y(z_hi, d).start()
 
+    @pl.when(y == 0)
+    def _():
+        exchange2((z_hi + 1) % 4).start()
+
+    for o in order[2:]:
+        exchange2((z_hi + o) % 4).start()
+
     def share_corner(d):
         return pltpu.make_async_remote_copy(
             src_ref=tiles.at[quarter], dst_ref=tiles.at[quarter],
@@ -311,6 +321,18 @@
     def _():
         for i in range(4):
             tt[i] = f2[:, i * B : (i + 1) * B].T.reshape(16, CYC, B)
+
+    for q in range(4):
+
+        @pl.when(wide != 4 * q)
+        def _():
+            corner_from(q).wait_recv()
+
+    for d in (2, 3, 1):
+        share_corner(d).start()
+
+    @pl.when(z_hi != quarter)
+    def _():
         for o in (1, 3, 0):
             chunk = (z_hi + o) % 4
 
@@ -318,29 +340,6 @@
             def _():
                 for k in range(4):
                     spread_columns(4 * chunk + k).start()
-
-    def share_corner(d):
-        return pltpu.make_async_remote_copy(
-            src_ref=tiles.at[quarter], dst_ref=tiles.at[quarter],
-            send_sem=cs_send.at[d], recv_sem=cs_recv.at[quarter],
-            device_id=(cube ^ d, wide), device_id_type=MESH,
-        )
-
-    def corner_from(q):
-        return pltpu.make_async_remote_copy(
-            src_ref=tiles.at[quarter, q], dst_ref=tiles.at[quarter, q],
-            send_sem=co_send.at[0], recv_sem=co_recv.at[q],
-            device_id=(cube, 4 * q), device_id_type=MESH,
-        )
-
-    for q in range(4):
-
-        @pl.when(wide != 4 * q)
-        def _():
-            corner_from(q).wait_recv()
-
-    for d in (2, 3, 1):
-        share_corner(d).start()
 
     for o in (1, 3, 2):
         piece_z = (z_hi + o) % 4

time: 52.4 us -> 52.4 us (level)
  no operation moved by 1% of the time
where the time goes in v4:
time: 52.4 us; the launch traced here: 52.2 us
  Pallas kernels  50.3 us (96%)
  local copies, waits for them, and re-layouts  1.31 us (2%)
  between operations  0.64 us (1%)
    pallas_call x1, Pallas kernels, on_device(): pl.pallas_call(kernel, out_shape=(jax.ShapeDtypeStruct((1, PIV, B), F32),...  50.3 us
    unnamed x2, local copies, waits for them, and re-layouts  1.31 us

profile of v4, /device:TPU:1, one launch (start us, length us, event | category | flops | bytes accessed | tf_op | source)
XLA Modules:
  0.0 52.2 jit_solution(4237091897747812634)
XLA Ops:
  0.6 50.3 %shard_map.86 = (f32[1,32,128]{2,1,0:T(8,128)S(1)}, f32[128,1,512]{2,1,0:T(1,128)S(1)}) custom-call(f32[1,128,2048]{2,1,0:T(8,128)} %x_hbm.1, f32[128,1,2,512]{3,2,1,0:T(2,128)} %l1_hbm.1, f32[128,1,512]{2,1,0:T(1,128)} %l2_hbm.1, s32[32,2048]{1,0:T(8,128)} %lm_hbm.1, s32[16,32]{1,0:T(8,128)} %bitcast.1, s32[16,2048]{1,0:T(8,128)} %pm_hbm.1, s32[16,16]{1,0:T(8,128)} %pv_hbm.1), custom_call_target="tpu_custom_call" | custom-call | flops 600000000 | bytes 3000000 | tf_op jit(solution)/shard_map/pallas_call | solution.py:517
  50.9 0.6 %copy.11 = f32[1,32,128]{2,1,0:T(8,128)} copy(f32[1,32,128]{2,1,0:T(8,128)S(1)} %get-tuple-element.4) | data formatting | bytes 32768
  51.5 0.7 %copy.12 = f32[128,1,512]{2,1,0:T(1,128)} copy(f32[128,1,512]{2,1,0:T(1,128)S(1)} %get-tuple-element.5) | data formatting | bytes 524288

commit v5 on v4

--- a/solution.py
+++ b/solution.py
@@ -300,20 +300,24 @@
             device_id=(group + part, 4 * quarter + k), device_id_type=MESH,
         )
 
+    def start_rows(chunk):
+        @pl.when(by_rows(z_hi, quarter, chunk))
+        def _():
+            for k in range(4):
+                w = 4 * chunk + k
+
+                @pl.when(w != wide)
+                def _():
+                    spread_rows(w).start()
+
     for o in order:
         chunk = (z_hi + o) % 4
         exchange2(chunk).wait_recv()
         rows = pl.ds(pl.multiple_of(chunk * 32, 32), 32)
         f2[rows, :] = uk[rows, :] + ur[rows, :]
 
-        @pl.when(by_rows(z_hi, quarter, chunk))
-        def _():
-            for k in range(4):
-                w = 4 * chunk + k
-
-                @pl.when(w != wide)
-                def _():
-                    spread_rows(w).start()
+        if o in order[:2]:
+            start_rows(chunk)
 
     f2r[z_hi, y] = f2[rows_of(wide), :]
 
@@ -330,22 +334,25 @@
 
     for d in (2, 3, 1):
         share_corner(d).start()
-
-    @pl.when(z_hi != quarter)
-    def _():
-        for o in (1, 3, 0):
-            chunk = (z_hi + o) % 4
-
-            @pl.when(ring(z_hi, chunk) < ring(quarter, chunk))
-            def _():
-                for k in range(4):
-                    spread_columns(4 * chunk + k).start()
 
     for o in (1, 3, 2):
         piece_z = (z_hi + o) % 4
         piece_from(4 * piece_z + y).wait_recv()
         for d in (2, 1, 3):
             along_y(piece_z, d).start()
+
+    for o in order[2:]:
+        start_rows((z_hi + o) % 4)
+
+    @pl.when(z_hi != quarter)
+    def _():
+        for o in (1, 3, 0):
+            chunk = (z_hi + o) % 4
+
+            @pl.when(ring(z_hi, chunk) < ring(quarter, chunk))
+            def _():
+                for k in range(4):
+                    spread_columns(4 * chunk + k).start()
 
     for d in range(1, 4):
         other = quarter ^ d

time: 52.4 us -> 52.4 us (level)
  no operation moved by 1% of the time
where the time goes in v5:
time: 52.4 us; the launch traced here: 52.2 us
  Pallas kernels  50.3 us (96%)
  local copies, waits for them, and re-layouts  1.31 us (2%)
  between operations  0.64 us (1%)
    pallas_call x1, Pallas kernels, on_device(): pl.pallas_call(kernel, out_shape=(jax.ShapeDtypeStruct((1, PIV, B), F32),...  50.3 us
    unnamed x2, local copies, waits for them, and re-layouts  1.31 us

profile of v5, /device:TPU:1, one launch (start us, length us, event | category | flops | bytes accessed | tf_op | source)
XLA Modules:
  0.0 52.2 jit_solution(1172915139586384390)
XLA Ops:
  0.6 50.3 %shard_map.86 = (f32[1,32,128]{2,1,0:T(8,128)S(1)}, f32[128,1,512]{2,1,0:T(1,128)S(1)}) custom-call(f32[1,128,2048]{2,1,0:T(8,128)} %x_hbm.1, f32[128,1,2,512]{3,2,1,0:T(2,128)} %l1_hbm.1, f32[128,1,512]{2,1,0:T(1,128)} %l2_hbm.1, s32[32,2048]{1,0:T(8,128)} %lm_hbm.1, s32[16,32]{1,0:T(8,128)} %bitcast.1, s32[16,2048]{1,0:T(8,128)} %pm_hbm.1, s32[16,16]{1,0:T(8,128)} %pv_hbm.1), custom_call_target="tpu_custom_call" | custom-call | flops 600000000 | bytes 3000000 | tf_op jit(solution)/shard_map/pallas_call | solution.py:524
  50.9 0.6 %copy.11 = f32[1,32,128]{2,1,0:T(8,128)} copy(f32[1,32,128]{2,1,0:T(8,128)S(1)} %get-tuple-element.4) | data formatting | bytes 32768
  51.5 0.7 %copy.12 = f32[128,1,512]{2,1,0:T(1,128)} copy(f32[128,1,512]{2,1,0:T(1,128)S(1)} %get-tuple-element.5) | data formatting | bytes 524288

commit v6 on v5

--- a/solution.py
+++ b/solution.py
@@ -23,7 +23,7 @@
     x_hbm, l1_hbm, l2_hbm, lm_hbm, ll_hbm, pm_hbm, pv_hbm,
     panel_hbm, schur_hbm,
     x_v, l1_v, l2_v, lm_v, pm_v, ll_s, pv_s,
-    zs, zo, zr, us, uk, ur, f2, f2r, tt, at, lt, cr, terms, tiles, msgs, mat, linv, tr_v,
+    zs, zo, zr, us, uk, ur, f2, f2r, tt, at, lt, cr, terms, tiles, msgs, packs, mat, linv, tr_v,
     in_sem, e1_send, e1_recv, e2_send, e2_recv, aa_send, aa_recv, ac_send,
     cr_send, cr_recv, pa_send, pb_send, pa_recv, zg_send, yg_send, pg_recv, cb_send, cb_recv,
     co_send, co_recv, cs_send, cs_recv,
@@ -78,9 +78,10 @@
 
     greet(cube ^ 2, 4 * z_hi)
     for d in (2, 3, 1):
-        greet(cube ^ d, wide)
+        for e in range(4):
+            greet(cube ^ d, 4 * z_hi + (y + e) % 4)
     apart = ring(z_hi, quarter)
-    greetings = 18 + 4 * (apart % 2 * 2 + apart // 2) + 4 * (1 - (y + 3) // 4)
+    greetings = 27 + 4 * (apart % 2 * 2 + apart // 2) + 4 * (1 - (y + 3) // 4)
 
     def one_hot(map_ref, live_ref, live_row, block):
         lanes = pl.multiple_of(block * B, B)
@@ -341,6 +342,35 @@
         for d in (2, 1, 3):
             along_y(piece_z, d).start()
 
+    for e in range(4):
+        to_y = (y + e) % 4
+        packed = jnp.zeros((CYC, B), F32)
+        for r in range(4):
+            rows = at[rows_of(4 * r + y), :]
+            for i in range(4):
+                first = PIV * r + CYC * i
+                moved = pltpu.roll(rows[:, B * i : B * (i + 1)], (first + B - CYC * (4 * z_hi + to_y)) % B, 1)
+                packed = jnp.where(lane[:CYC] >= first, moved, packed)
+        packs[e] = packed
+
+    def share(d, e):
+        return pltpu.make_async_remote_copy(
+            src_ref=packs.at[e], dst_ref=msgs.at[quarter, y], send_sem=cb_send.at[d, e], recv_sem=cb_recv.at[quarter, y],
+            device_id=(cube ^ d, 4 * z_hi + (y + e) % 4), device_id_type=MESH,
+        )
+
+    def shared_from(d, e):
+        other, other_y = quarter ^ d, (y + e) % 4
+        return pltpu.make_async_remote_copy(
+            src_ref=packs.at[0], dst_ref=msgs.at[other, other_y], send_sem=cb_send.at[d, e], recv_sem=cb_recv.at[other, other_y],
+            device_id=(group + other, 4 * z_hi + other_y), device_id_type=MESH,
+        )
+
+    others = [(d, e) for d in (2, 3, 1, 0) for e in (2, 1, 3, 0) if d or e]
+    for d, e in others:
+        share(d, e).start()
+    msgs[quarter, y] = packs[0]
+
     for o in order[2:]:
         start_rows((z_hi + o) % 4)
 
@@ -378,34 +408,8 @@
             mat[PIV * q + CYC * r : PIV * q + CYC * (r + 1), :B] = got[CYC * q : CYC * (q + 1)]
     mat[:, B:] = jnp.where(iota((B, B), 0) == lane, 1.0, 0.0)
 
-    def share(d):
-        return pltpu.make_async_remote_copy(
-            src_ref=msgs.at[quarter], dst_ref=msgs.at[quarter],
-            send_sem=cb_send.at[d], recv_sem=cb_recv.at[quarter],
-            device_id=(cube ^ d, wide), device_id_type=MESH,
-        )
-
     @pl.loop(0, 4)
     def _(step):
-        @pl.when(step == 2)
-        def _():
-            @pl.loop(0, 16)
-            def _(piece):
-                @pl.when(piece % 4 != y)
-                def _():
-                    piece_from(piece).wait_recv()
-
-            packed = jnp.zeros((PIV, B), F32)
-            for r in range(4):
-                for i in range(4):
-                    first = PIV * r + CYC * i
-                    part = at[PIV * r : PIV * (r + 1), B * i : B * (i + 1)]
-                    moved = pltpu.roll(part, (first + B - CYC * wide) % B, 1)
-                    packed = jnp.where(lane[:PIV] >= first, moved, packed)
-            msgs[quarter] = packed
-            for d in (2, 3, 1):
-                share(d).start()
-
         left = mat[:PIV, :B]
         right = mat[:PIV, B:]
         row_id = iota((PIV, B), 0)
@@ -438,19 +442,20 @@
             mat[: B - PIV, :B] = trail_left - change[: B - PIV, :B]
             mat[: B - PIV, B:] = trail_right - change[: B - PIV, B:]
 
+    @pl.loop(0, 16)
+    def _(piece):
+        @pl.when(piece % 4 != y)
+        def _():
+            piece_from(piece).wait_recv()
+
     lower = linv[...]
     lt[...] = jnp.dot(lower, at[...], precision=HIGHEST, preferred_element_type=F32)
     tr_v[...] = lt[:, pl.ds(pl.multiple_of(wide // 4 * B, B), B)].T
     panel_hbm[0] = tr_v[pl.ds(pl.multiple_of(wide % 4 * PIV, PIV), PIV), :]
-    for d in range(1, 4):
-        other = quarter ^ d
-        pltpu.make_async_remote_copy(
-            src_ref=msgs.at[other], dst_ref=msgs.at[other],
-            send_sem=cb_send.at[d], recv_sem=cb_recv.at[other],
-            device_id=(group + other, wide), device_id_type=MESH,
-        ).wait_recv()
-
-    shared = [msgs[c] for c in range(4)]
+    for d, e in others:
+        shared_from(d, e).wait_recv()
+
+    shared = [msgs[c].reshape(PIV, B) for c in range(4)]
     rows_t = jnp.concatenate([gathered(shared, r) for r in range(4)], axis=0)
     own_t = jnp.dot(lower, rows_t, precision=HIGHEST, preferred_element_type=F32)
     update = lax.dot_general(
@@ -493,10 +498,12 @@
 
     for d in range(1, 4):
         along_z(d).wait_send()
-        share(d).wait_send()
         share_corner(d).wait_send()
         for piece_z in range(4):
             along_y(piece_z, d).wait_send()
+
+    for d, e in others:
+        share(d, e).wait_send()
 
     for o in range(4):
         chunk = (z_hi + o) % 4
@@ -537,10 +544,10 @@
             vmem((B, Q), F32), vmem((B, Q), F32), vmem((B, Q), F32), vmem((B, Q), F32),
             vmem((4, 4, CYC, Q), F32), vmem((4, 16, CYC, B), F32), vmem((B, Q), F32), vmem((B, Q), F32),
             vmem((PIV, B), F32), vmem((2, CYC, Q), F32),
-            vmem((4, 4, CYC, B), F32), vmem((4, PIV, B), F32), vmem((B, 2 * B), F32), vmem((B, B), F32),
+            vmem((4, 4, CYC, B), F32), vmem((4, 4, CYC, B), F32), vmem((4, CYC, B), F32), vmem((B, 2 * B), F32), vmem((B, B), F32),
             vmem((B, B), F32),
             dma((7,)), dma((2,)), dma((2,)), dma((4,)), dma((4,)), dma((16,)), dma((16,)), dma((16,)),
-            dma, dma, dma((4,)), dma((4,)), dma((2,)), dma((4,)), dma((4, 4)), dma((16,)), dma((4,)), dma((4,)),
+            dma, dma, dma((4,)), dma((4,)), dma((2,)), dma((4,)), dma((4, 4)), dma((16,)), dma((4, 4)), dma((4, 4)),
             dma((16,)), dma((4,)), dma((4,)), dma((4,)),
         ],
         compiler_params=pltpu.CompilerParams(

time: 52.4 us -> 52.3 us (level)
  no operation moved by 1% of the time
where the time goes in v6:
time: 52.3 us; the launch traced here: 52.1 us
  Pallas kernels  50.2 us (96%)
  local copies, waits for them, and re-layouts  1.31 us (3%)
  between operations  0.64 us (1%)
    pallas_call x1, Pallas kernels, on_device(): pl.pallas_call(kernel, out_shape=(jax.ShapeDtypeStruct((1, PIV, B), F32),...  50.2 us
    unnamed x2, local copies, waits for them, and re-layouts  1.31 us

profile of v6, /device:TPU:1, one launch (start us, length us, event | category | flops | bytes accessed | tf_op | source)
XLA Modules:
  0.0 52.1 jit_solution(8110077730932068341)
XLA Ops:
  0.6 50.2 %shard_map.86 = (f32[1,32,128]{2,1,0:T(8,128)S(1)}, f32[128,1,512]{2,1,0:T(1,128)S(1)}) custom-call(f32[1,128,2048]{2,1,0:T(8,128)} %x_hbm.1, f32[128,1,2,512]{3,2,1,0:T(2,128)} %l1_hbm.1, f32[128,1,512]{2,1,0:T(1,128)} %l2_hbm.1, s32[32,2048]{1,0:T(8,128)} %lm_hbm.1, s32[16,32]{1,0:T(8,128)} %bitcast.1, s32[16,2048]{1,0:T(8,128)} %pm_hbm.1, s32[16,16]{1,0:T(8,128)} %pv_hbm.1), custom_call_target="tpu_custom_call" | custom-call | flops 600000000 | bytes 3000000 | tf_op jit(solution)/shard_map/pallas_call | solution.py:531
  50.8 0.6 %copy.11 = f32[1,32,128]{2,1,0:T(8,128)} copy(f32[1,32,128]{2,1,0:T(8,128)S(1)} %get-tuple-element.4) | data formatting | bytes 32768
  51.4 0.7 %copy.12 = f32[128,1,512]{2,1,0:T(1,128)} copy(f32[128,1,512]{2,1,0:T(1,128)S(1)} %get-tuple-element.5) | data formatting | bytes 524288

commit v7 on v6

--- a/solution.py
+++ b/solution.py
@@ -317,8 +317,6 @@
         rows = pl.ds(pl.multiple_of(chunk * 32, 32), 32)
         f2[rows, :] = uk[rows, :] + ur[rows, :]
 
-        if o in order[:2]:
-            start_rows(chunk)
 
     f2r[z_hi, y] = f2[rows_of(wide), :]
 
@@ -371,7 +369,7 @@
         share(d, e).start()
     msgs[quarter, y] = packs[0]
 
-    for o in order[2:]:
+    for o in order:
         start_rows((z_hi + o) % 4)
 
     @pl.when(z_hi != quarter)

time: 52.3 us -> 50.2 us (0.960)
  Pallas kernels: 50.2 us -> 47.9 us
    pallas_call x1, Pallas kernels: 50.2 us -> 47.9 us  [on_device(): pl.pallas_call(kernel, out_shape=(jax.ShapeDtypeStruct((1, PIV, B), F32),...]
where the time goes in v7:
time: 50.2 us; the launch traced here: 49.8 us
  Pallas kernels  47.9 us (95%)
  local copies, waits for them, and re-layouts  1.31 us (3%)
  between operations  0.64 us (1%)
    pallas_call x1, Pallas kernels, on_device(): pl.pallas_call(kernel, out_shape=(jax.ShapeDtypeStruct((1, PIV, B), F32),...  47.9 us
    unnamed x2, local copies, waits for them, and re-layouts  1.31 us

profile of v7, /device:TPU:1, one launch (start us, length us, event | category | flops | bytes accessed | tf_op | source)
XLA Modules:
  0.0 49.8 jit_solution(12527159366827148599)
XLA Ops:
  0.6 47.9 %shard_map.86 = (f32[1,32,128]{2,1,0:T(8,128)S(1)}, f32[128,1,512]{2,1,0:T(1,128)S(1)}) custom-call(f32[1,128,2048]{2,1,0:T(8,128)} %x_hbm.1, f32[128,1,2,512]{3,2,1,0:T(2,128)} %l1_hbm.1, f32[128,1,512]{2,1,0:T(1,128)} %l2_hbm.1, s32[32,2048]{1,0:T(8,128)} %lm_hbm.1, s32[16,32]{1,0:T(8,128)} %bitcast.1, s32[16,2048]{1,0:T(8,128)} %pm_hbm.1, s32[16,16]{1,0:T(8,128)} %pv_hbm.1), custom_call_target="tpu_custom_call" | custom-call | flops 600000000 | bytes 3000000 | tf_op jit(solution)/shard_map/pallas_call | solution.py:529
  48.5 0.6 %copy.11 = f32[1,32,128]{2,1,0:T(8,128)} copy(f32[1,32,128]{2,1,0:T(8,128)S(1)} %get-tuple-element.4) | data formatting | bytes 32768
  49.1 0.7 %copy.12 = f32[128,1,512]{2,1,0:T(1,128)} copy(f32[128,1,512]{2,1,0:T(1,128)S(1)} %get-tuple-element.5) | data formatting | bytes 524288

commit v8 on v7

--- a/solution.py
+++ b/solution.py
@@ -369,7 +369,7 @@
         share(d, e).start()
     msgs[quarter, y] = packs[0]
 
-    for o in order:
+    for o in order[:3]:
         start_rows((z_hi + o) % 4)
 
     @pl.when(z_hi != quarter)
@@ -381,6 +381,8 @@
             def _():
                 for k in range(4):
                     spread_columns(4 * chunk + k).start()
+
+    start_rows(z_hi)
 
     for d in range(1, 4):
         other = quarter ^ d

time: 50.2 us -> 50.2 us (level)
  no operation moved by 1% of the time
where the time goes in v8:
time: 50.2 us; the launch traced here: 49.8 us
  Pallas kernels  47.9 us (95%)
  local copies, waits for them, and re-layouts  1.31 us (3%)
  between operations  0.64 us (1%)
    pallas_call x1, Pallas kernels, on_device(): pl.pallas_call(kernel, out_shape=(jax.ShapeDtypeStruct((1, PIV, B), F32),...  47.9 us
    unnamed x2, local copies, waits for them, and re-layouts  1.31 us

profile of v8, /device:TPU:1, one launch (start us, length us, event | category | flops | bytes accessed | tf_op | source)
XLA Modules:
  0.0 49.8 jit_solution(15823876850704974527)
XLA Ops:
  0.6 47.9 %shard_map.86 = (f32[1,32,128]{2,1,0:T(8,128)S(1)}, f32[128,1,512]{2,1,0:T(1,128)S(1)}) custom-call(f32[1,128,2048]{2,1,0:T(8,128)} %x_hbm.1, f32[128,1,2,512]{3,2,1,0:T(2,128)} %l1_hbm.1, f32[128,1,512]{2,1,0:T(1,128)} %l2_hbm.1, s32[32,2048]{1,0:T(8,128)} %lm_hbm.1, s32[16,32]{1,0:T(8,128)} %bitcast.1, s32[16,2048]{1,0:T(8,128)} %pm_hbm.1, s32[16,16]{1,0:T(8,128)} %pv_hbm.1), custom_call_target="tpu_custom_call" | custom-call | flops 600000000 | bytes 3000000 | tf_op jit(solution)/shard_map/pallas_call | solution.py:531
  48.5 0.6 %copy.11 = f32[1,32,128]{2,1,0:T(8,128)} copy(f32[1,32,128]{2,1,0:T(8,128)S(1)} %get-tuple-element.4) | data formatting | bytes 32768
  49.1 0.7 %copy.12 = f32[128,1,512]{2,1,0:T(1,128)} copy(f32[128,1,512]{2,1,0:T(1,128)S(1)} %get-tuple-element.5) | data formatting | bytes 524288

commit v9 on v7

--- a/solution.py
+++ b/solution.py
@@ -418,7 +418,9 @@
                 j = first + n
                 pivot = columns[n][j : j + 1, :]
                 diag = jnp.where(row_id == j, pivot, diag)
-                factor = jnp.where(row_id > j, columns[n] * (1.0 / pivot), 0.0)
+                inverse = pl.reciprocal(pivot, approx=True)
+                inverse = inverse * (2.0 - pivot * inverse)
+                factor = jnp.where(row_id > j, columns[n] * inverse, 0.0)
                 for m in range(n + 1, CYC):
                     columns[m] = columns[m] - factor * columns[m][j : j + 1, :]
                 left = left - factor * left[j : j + 1, :]

time: 50.2 us -> 50.2 us (level)
  no operation moved by 1% of the time
where the time goes in v9:
time: 50.2 us; the launch traced here: 50 us
  Pallas kernels  48.1 us (96%)
  local copies, waits for them, and re-layouts  1.31 us (3%)
  between operations  0.64 us (1%)
    pallas_call x1, Pallas kernels, on_device(): pl.pallas_call(kernel, out_shape=(jax.ShapeDtypeStruct((1, PIV, B), F32),...  48.1 us
    unnamed x2, local copies, waits for them, and re-layouts  1.31 us

profile of v9, /device:TPU:1, one launch (start us, length us, event | category | flops | bytes accessed | tf_op | source)
XLA Modules:
  0.0 50.0 jit_solution(4410331890922344475)
XLA Ops:
  0.6 48.1 %shard_map.86 = (f32[1,32,128]{2,1,0:T(8,128)S(1)}, f32[128,1,512]{2,1,0:T(1,128)S(1)}) custom-call(f32[1,128,2048]{2,1,0:T(8,128)} %x_hbm.1, f32[128,1,2,512]{3,2,1,0:T(2,128)} %l1_hbm.1, f32[128,1,512]{2,1,0:T(1,128)} %l2_hbm.1, s32[32,2048]{1,0:T(8,128)} %lm_hbm.1, s32[16,32]{1,0:T(8,128)} %bitcast.1, s32[16,2048]{1,0:T(8,128)} %pm_hbm.1, s32[16,16]{1,0:T(8,128)} %pv_hbm.1), custom_call_target="tpu_custom_call" | custom-call | flops 600000000 | bytes 3000000 | tf_op jit(solution)/shard_map/pallas_call | solution.py:531
  48.7 0.6 %copy.11 = f32[1,32,128]{2,1,0:T(8,128)} copy(f32[1,32,128]{2,1,0:T(8,128)S(1)} %get-tuple-element.4) | data formatting | bytes 32768
  49.3 0.7 %copy.12 = f32[128,1,512]{2,1,0:T(1,128)} copy(f32[128,1,512]{2,1,0:T(1,128)S(1)} %get-tuple-element.5) | data formatting | bytes 524288
